TPU v7x, 512 devices: a whole 4x8x8 slice. The times are simulated.
512 devices in a mesh: pool: 64 (over x, y, core), tp: 8 (over z).
Axes of the slice: x: 4, y: 8, z: 8, core: 2. Of those that a mesh axis runs over, the one named last changes fastest.
Arguments:
- queries: bfloat16 [64, 6144], P('pool', 'tp'), may hold values from -6 to 6
- suffix_keys: bfloat16 [64, 1024], P('pool', 'tp'), may hold values from -15 to 15
- suffix_values: bfloat16 [64, 1024], P('pool', 'tp'), may hold values from -6 to 6
- prefix_keys: bfloat16 [1024, 128, 1024], P('pool', None, 'tp'), may hold values from -16 to 16
- prefix_values: bfloat16 [1024, 128, 1024], P('pool', None, 'tp'), may hold values from -6 to 6
- block_slot: int32 [2, 256], replicated, may hold values from 0 to 1023, as said below
- suffix_len: int32 [2], replicated, may hold values from 8 to 32, as said below
- out_weight: bfloat16 [6144, 12288], P('tp', 'pool'), may hold values from -0.078125 to 0.078125
Outputs:
- attn_out: bfloat16 [64, 12288], P('tp', 'pool')
Inputs may be any that keep to these rules, and one draw needn't show every extreme that they name: `block_slot`: the 512 entries are distinct slots owner * 16 + k; the blocks of each owner fill its slots k = 0 to its count - 1, counts differ between owners, and some owners have all 16 slots in use. `suffix_len`: some conversation has all 32 positions live.
All inputs are finite; a program needn't handle non-finite values.
Results may differ from a plain program's by a relative error of at most 0.019.
Values may be sent and summed in bfloat16 or wider, within the bound.
A program may use at most 64 MiB of HBM per device.

v0:
```python
import math

import jax
import jax.numpy as jnp
from jax import lax
from jax.sharding import PartitionSpec as P

H = 48
KVH = 8
HD = 128
CONV = 2
SUF = 32


NEG_FILL = -1e30


def block_terms(query_rows, key_rows, value_rows, score_scale, allowed):
    scores = (
        jnp.einsum("rnge,kne->rngk", query_rows, key_rows, preferred_element_type=jnp.float32)
        * score_scale
    )
    if allowed is not None:
        scores = jnp.where(allowed, scores, NEG_FILL)
    block_max = jnp.max(scores, axis=-1)
    powers = jnp.exp(scores - block_max[..., None])
    block_sum = jnp.sum(powers, axis=-1)
    block_out = jnp.einsum(
        "rngk,kne->rnge",
        powers.astype(jnp.bfloat16),
        value_rows,
        preferred_element_type=jnp.float32,
    )
    return (block_max, block_sum, block_out)


def join(earlier, later):
    row_max = jnp.maximum(earlier[0], later[0])
    early_scale = jnp.exp(earlier[0] - row_max)
    late_scale = jnp.exp(later[0] - row_max)
    row_total = early_scale * earlier[1] + late_scale * later[1]
    numerator = early_scale[..., None] * earlier[2] + late_scale[..., None] * later[2]
    return (row_max, row_total, numerator)


def fold_rows(received):
    row_max = jnp.max(received[0], axis=0)
    scales = jnp.exp(received[0] - row_max[None])
    row_total = jnp.sum(scales * received[1], axis=0)
    numerator = jnp.sum(scales[..., None] * received[2], axis=0)
    return (row_max, row_total, numerator)


def suffix_terms(query_rows, first_row, key_rows, value_rows, score_scale):
    row_pos = first_row + jnp.arange(query_rows.shape[0], dtype=jnp.int32)
    key_pos = jnp.arange(key_rows.shape[0], dtype=jnp.int32)
    allowed = (key_pos[None, :] <= row_pos[:, None]) & (
        key_pos[None, :] // SUF == row_pos[:, None] // SUF
    )
    return block_terms(query_rows, key_rows, value_rows, score_scale, allowed[:, None, None, :])


def finish(parts, first_row, suffix_len):
    count_rows = parts[2].shape[0]
    values_out = parts[2] / parts[1][..., None]
    positions = first_row + jnp.arange(count_rows, dtype=jnp.int32)
    dialog = positions // SUF
    offset = positions - dialog * SUF
    matches = dialog[:, None] == jnp.arange(CONV, dtype=jnp.int32)[None, :]
    limits = jnp.sum(jnp.where(matches, suffix_len[None, :], 0), axis=1)
    alive_rows = offset < limits
    shaped = jnp.where(alive_rows[:, None, None, None], values_out, 0.0)
    return shaped.reshape(count_rows, -1).astype(jnp.bfloat16)


def shards(
    queries,
    suffix_keys,
    suffix_values,
    prefix_keys,
    prefix_values,
    block_slot,
    suffix_len,
    out_weight,
):
    owner_index = lax.axis_index("pool")
    rows_here = queries.shape[0]
    heads_kv = suffix_keys.shape[1] // HD
    groups = H // KVH
    score_scale = 1.0 / math.sqrt(HD)
    all_queries, all_keys, all_values = (
        lax.all_gather(queries, "pool", axis=0, tiled=True),
        lax.all_gather(suffix_keys, "pool", axis=0, tiled=True),
        lax.all_gather(suffix_values, "pool", axis=0, tiled=True),
    )
    tokens_all = all_queries.shape[0]
    query_blocks = all_queries.reshape(CONV, SUF, heads_kv, groups, HD)
    capacity = prefix_keys.shape[0]
    block_len = prefix_keys.shape[1]
    slot_list = block_slot.reshape(-1)
    dialog_ids = jnp.arange(slot_list.shape[0], dtype=jnp.int32) // block_slot.shape[1]
    wanted = owner_index * capacity + jnp.arange(capacity, dtype=jnp.int32)
    matches = (slot_list[None, :] == wanted[:, None]).astype(jnp.int32)
    used_slots = jnp.sum(matches)
    slot_dialog = jnp.sum(matches * dialog_ids[None, :], axis=1)

    def visit(slot_index, carry_state):
        dialog = slot_dialog[slot_index]
        query_rows = lax.dynamic_index_in_dim(query_blocks, dialog, 0, keepdims=False)
        key_rows = lax.dynamic_index_in_dim(prefix_keys, slot_index, 0, keepdims=False).reshape(
            block_len, heads_kv, HD
        )
        value_rows = lax.dynamic_index_in_dim(prefix_values, slot_index, 0, keepdims=False).reshape(
            block_len, heads_kv, HD
        )
        current = block_terms(query_rows, key_rows, value_rows, score_scale, None)
        before = (
            lax.dynamic_index_in_dim(carry_state[0], dialog, 0, keepdims=False),
            lax.dynamic_index_in_dim(carry_state[1], dialog, 0, keepdims=False),
            lax.dynamic_index_in_dim(carry_state[2], dialog, 0, keepdims=False),
        )
        after = join(before, current)
        return (
            lax.dynamic_update_index_in_dim(carry_state[0], after[0], dialog, 0),
            lax.dynamic_update_index_in_dim(carry_state[1], after[1], dialog, 0),
            lax.dynamic_update_index_in_dim(carry_state[2], after[2], dialog, 0),
        )

    start = (
        jnp.full((CONV, SUF, heads_kv, groups), NEG_FILL, jnp.float32),
        jnp.zeros((CONV, SUF, heads_kv, groups), jnp.float32),
        jnp.zeros((CONV, SUF, heads_kv, groups, HD), jnp.float32),
    )
    local_state = lax.fori_loop(0, used_slots, visit, start)
    key_rows_all = all_keys.reshape(tokens_all, heads_kv, HD)
    value_rows_all = all_values.reshape(tokens_all, heads_kv, HD)
    outgoing = (
        local_state[0].reshape(1, tokens_all, heads_kv, groups),
        local_state[1].reshape(1, tokens_all, heads_kv, groups),
        local_state[2].reshape(1, tokens_all, heads_kv, groups, HD),
    )
    received = (
        lax.all_to_all(outgoing[0], "pool", split_axis=1, concat_axis=0, tiled=True),
        lax.all_to_all(outgoing[1], "pool", split_axis=1, concat_axis=0, tiled=True),
        lax.all_to_all(outgoing[2], "pool", split_axis=1, concat_axis=0, tiled=True),
    )
    prefix_part = fold_rows(received)
    first_row = owner_index * rows_here
    own_queries = queries.reshape(rows_here, heads_kv, groups, HD)
    suffix_part = suffix_terms(own_queries, first_row, key_rows_all, value_rows_all, score_scale)
    attn_rows = finish(join(prefix_part, suffix_part), first_row, suffix_len)
    attention = lax.all_gather(attn_rows, "pool", axis=0, tiled=True)
    return lax.psum_scatter(
        jnp.dot(attention, out_weight, preferred_element_type=jnp.float32).astype(jnp.bfloat16),
        "tp",
        scatter_dimension=0,
        tiled=True,
    )


def solution(mesh):
    in_specs = (
        P("pool", "tp"),
        P("pool", "tp"),
        P("pool", "tp"),
        P("pool", None, "tp"),
        P("pool", None, "tp"),
        P(),
        P(),
        P("tp", "pool"),
    )
    out_specs = P("tp", "pool")
    return jax.shard_map(shards, mesh=mesh, in_specs=in_specs, out_specs=out_specs, check_vma=False)
```

profile of v0, /device:TPU:2, one launch (start us, length us, event | category | flops | bytes accessed | tf_op | source)
XLA Modules:
  0.0 332.0 jit_solution(11568403610672097986)
XLA Ops:
  6.5 0.7 copy-done.2
  7.3 0.7 copy-done.1
  8.0 41.0 %all-gather = bf16[64,1,768]{2,1,0:T(2,128)(2,1)S(1)} all-gather(bf16[1,1,768]{2,1,0:T(2,128)(2,1)S(1)} %bitcast.190), channel_id=1, replica_groups=mesh['pool'=64,'tp'=8] {'pool'}, dimensions={0}, use_global_device_ids=true | all-gather | bytes 99840 | tf_op jit(solution)/shard_map/all_gather | solution.py:92
  49.7 0.7 fusion.37
  50.5 54.1 %while.14 = (s32[]{:T(128)}, f32[2,32,1,6]{1,3,2,0:T(8,128)S(1)}, f32[2,32,1,6]{1,3,2,0:T(8,128)S(1)}, f32[2,32,1,6,128]{4,1,0,3,2:T(8,128)S(1)}, s32[]{:T(128)}...) while((s32[]{:T(128)}, f32[2,32,1,6]{1,3,2,0:T(8,128)S(1)}, ...), condition=%wide.region_6.7_spmd, body=%wide.region_3.6_spmd.sunk | while | flops 12805448 | bytes 845289 | solution.py:134
  53.6 1.0 fusion.71
  54.6 1.0 fusion.75
  56.4 0.6 dynamic_slice.62
  58.9 1.0 fusion.71
  60.0 1.0 fusion.75
  61.8 0.6 dynamic_slice.62
  64.3 1.0 fusion.71
  65.3 1.0 fusion.75
  67.1 0.6 dynamic_slice.62
  69.6 1.0 fusion.71
  70.7 1.0 fusion.75
  72.5 0.6 dynamic_slice.62
  75.0 1.0 fusion.71
  76.1 1.0 fusion.75
  80.3 1.0 fusion.71
  81.4 1.0 fusion.75
  83.2 0.6 dynamic_slice.62
  85.7 1.0 fusion.71
  86.8 1.0 fusion.75
  88.5 0.6 dynamic_slice.62
  91.1 1.0 fusion.71
  92.1 1.0 fusion.75
  93.9 0.6 dynamic_slice.62
  96.4 1.0 fusion.71
  97.5 1.0 fusion.75
  101.8 1.0 fusion.71
  102.8 1.0 fusion.75
  104.6 0.7 copy.55
  105.3 38.4 %all-to-all-start = ((f32[1,64,1,6]{3,2,0,1:T(1,128)}), f32[1,64,1,6]{3,2,0,1:T(1,128)S(1)}, u32[]{:S(2)}, u32[]{:S(2)}) async-start(f32[1,64,1,6]{3,2,0,1:T(1,128)} %bitcast.22), calls=%async_computation | async-start | bytes 65536 | tf_op jit(solution)/shard_map/all_to_all | solution.py:143
  143.7 0.6 copy-done.3
  144.4 34.8 %all-gather.1 = bf16[64,1,128]{2,1,0:T(2,128)(2,1)S(1)} all-gather(bf16[1,1,128]{2,1,0:T(2,128)(2,1)S(1)} %bitcast.193), channel_id=1, replica_groups=mesh['pool'=64,'tp'=8] {'pool'}, dimensions={0}, use_global_device_ids=true | all-gather | bytes 16640 | tf_op jit(solution)/shard_map/all_gather | solution.py:93
  179.7 0.6 copy-done.5
  180.3 0.7 fusion.56
  181.0 0.7 copy.56
  181.7 0.9 copy.50
  183.2 8.2 %all-to-all-start.2 = ((f32[1,64,1,6]{3,2,0,1:T(1,128)}), f32[1,64,1,6]{3,2,0,1:T(1,128)S(1)}, u32[]{:S(2)}, u32[]{:S(2)}) async-start(f32[1,64,1,6]{3,2,0,1:T(1,128)} %bitcast.38), calls=%async_computation.2 | async-start | bytes 65536 | tf_op jit(solution)/shard_map/all_to_all | solution.py:144
  191.4 0.6 copy-done.4
  192.1 34.8 %all-gather.2 = bf16[64,1,128]{2,1,0:T(2,128)(2,1)S(1)} all-gather(bf16[1,1,128]{2,1,0:T(2,128)(2,1)S(1)} %bitcast.194), channel_id=1, replica_groups=mesh['pool'=64,'tp'=8] {'pool'}, dimensions={0}, use_global_device_ids=true | all-gather | bytes 16640 | tf_op jit(solution)/shard_map/all_gather | solution.py:94
  227.1 8.2 %all-to-all-start.1 = ((f32[1,64,1,6,128]{4,2,3,0,1:T(1,128)}), f32[1,64,1,6,128]{4,2,3,0,1:T(1,128)S(1)}, u32[]{:S(2)}, u32[]{:S(2)}) async-start(f32[1,64,1,6,128]{4,2,3,0,1:T(1,128)} %copy.50), calls=%async_computation.1 | async-start | bytes 393216 | tf_op jit(solution)/shard_map/all_to_all | solution.py:145
  235.9 9.6 %all-to-all-done.1 = f32[1,64,1,6,128]{4,2,3,0,1:T(1,128)S(1)} async-done(((f32[1,64,1,6,128]{4,2,3,0,1:T(1,128)}), f32[1,64,1,6,128]{4,2,3,0,1:T(1,128)S(1)}, u32[]{:S(2)}, u32[]{:S(2)}) %all-to-all-start.1) | async-done | bytes 196640 | tf_op jit(solution)/shard_map/all_to_all | solution.py:145
  246.2 36.9 %all-gather.3 = bf16[64,1,768]{2,1,0:T(2,128)(2,1)S(1)} all-gather(bf16[1,1,768]{2,1,0:T(2,128)(2,1)S(1)} %reshape.416), channel_id=1, replica_groups=mesh['pool'=64,'tp'=8] {'pool'}, dimensions={0}, use_global_device_ids=true | all-gather | bytes 99840 | tf_op jit(solution)/shard_map/all_gather | solution.py:152
  283.1 0.8 convolution_convert_fusion
  284.0 41.2 %reduce-scatter.2.cloned.1.call-done = bf16[8,192]{1,0:T(8,128)(2,1)} async-done(((bf16[64,192]{1,0:T(8,128)(2,1)}), bf16[8,192]{1,0:T(8,128)(2,1)}) %reduce-scatter.2.cloned.1.call-update) | async-done | bytes 3088 | tf_op jit(solution)/shard_map/reduce_scatter | solution.py:153
  (78 shorter events, 6.8 us)
Async XLA Ops:
  6.5 276.5 %copy-start = (bf16[768,192]{0,1:T(8,128)(2,1)S(1)}, bf16[768,192]{0,1:T(8,128)(2,1)}, u32[]{:S(2)}) copy-start(bf16[768,192]{0,1:T(8,128)(2,1)} %param.17) | copy-start | bytes 884740
  6.5 0.7 copy-start.2
  7.3 0.7 copy-start.1
  105.3 77.9 %all-to-all-start = ((f32[1,64,1,6]{3,2,0,1:T(1,128)}), f32[1,64,1,6]{3,2,0,1:T(1,128)S(1)}, u32[]{:S(2)}, u32[]{:S(2)}) async-start(f32[1,64,1,6]{3,2,0,1:T(1,128)} %bitcast.22), calls=%async_computation | async-start | bytes 65536 | tf_op jit(solution)/shard_map/all_to_all | solution.py:143
  143.7 0.7 copy-start.3
  179.6 0.7 copy-start.5
  183.2 43.9 %all-to-all-start.2 = ((f32[1,64,1,6]{3,2,0,1:T(1,128)}), f32[1,64,1,6]{3,2,0,1:T(1,128)S(1)}, u32[]{:S(2)}, u32[]{:S(2)}) async-start(f32[1,64,1,6]{3,2,0,1:T(1,128)} %bitcast.38), calls=%async_computation.2 | async-start | bytes 65536 | tf_op jit(solution)/shard_map/all_to_all | solution.py:144
  191.4 0.7 copy-start.4
  227.1 18.4 %all-to-all-start.1 = ((f32[1,64,1,6,128]{4,2,3,0,1:T(1,128)}), f32[1,64,1,6,128]{4,2,3,0,1:T(1,128)S(1)}, u32[]{:S(2)}, u32[]{:S(2)}) async-start(f32[1,64,1,6,128]{4,2,3,0,1:T(1,128)} %copy.50), calls=%async_computation.1 | async-start | bytes 393216 | tf_op jit(solution)/shard_map/all_to_all | solution.py:145
  235.3 89.8 %reduce-scatter.2.cloned.1.call-start = ((), (), s32[]{:S(2)}) async-start(), calls=%async_computation.4 | async-start | bytes 36864 | tf_op jit(solution)/shard_map/reduce_scatter | solution.py:153
Sparse Core Ops, SparseCore 0:
  284.1 41.0 reduce-scatter.1
where the time goes:
time: 335 us; the launch traced here: 332 us
  blocking collectives  148 us (44%)
  starting transfers between devices  54.8 us (16%)
  waiting for transfers between devices  50.8 us (15%)
  loops' own time  25.9 us (8%)
  matrix products  21.1 us (6%)
  between operations  14.2 us (4%)
  local copies, waits for them, and re-layouts  12.4 us (4%)
  other arithmetic  5.17 us (2%)
    reduce_scatter x1, waiting for transfers between devices, shards(): lax.psum_scatter(jnp.dot(attention, out_weight, preferred_element_type=jn...  41.2 us
    all_gather x1, blocking collectives, shards(): lax.all_gather(queries, 'pool', axis=0, tiled=True)  41 us
    all_to_all x1, starting transfers between devices, shards(): lax.all_to_all(outgoing[0], 'pool', split_axis=1, concat_axis=0, tiled=True)  38.4 us
    all_gather x1, blocking collectives, shards(): attention = lax.all_gather(attn_rows, 'pool', axis=0, tiled=True)  36.9 us
    all_gather x1, blocking collectives, shards(): lax.all_gather(suffix_keys, 'pool', axis=0, tiled=True)  34.8 us
    all_gather x1, blocking collectives, shards(): lax.all_gather(suffix_values, 'pool', axis=0, tiled=True)  34.8 us
    another operation x1, loops' own time, shards(): local_state = lax.fori_loop(0, used_slots, visit, start)  25.9 us
    dot_general x11, matrix products, block_terms(): jnp.einsum('rnge,kne->rngk', query_rows, key_rows, preferred_element_type...  10.3 us
  transfers between devices with their start and end apart: 4, of which 2 were waited for; matrix products, arithmetic and copies ran while one was open for 1% of the time, Pallas kernels for 0%

commit v1 on v0

v1 whole, which is shorter than its diff:
```python
import functools
import math

import jax
import jax.numpy as jnp
from jax import lax
from jax.experimental import pallas as pl
from jax.experimental.pallas import tpu as pltpu
from jax.sharding import PartitionSpec as P

H = 48
KVH = 8
HD = 128
CONV = 2
SUF = 32
GROUPS = H // KVH
ROWS = GROUPS * SUF
NEG = -1e30
EXP_SCALE = math.log2(math.e) / math.sqrt(HD)
MESH = pl.DeviceIdType.MESH

NX = 4
NY = 8
CHIPS = NX * NY
TP = 8
PAIRS = 16


def far_first(count, step):
    half = count // 2
    return half + (1 - 2 * lax.rem(step, 2)) * lax.div(step + 1, 2)


def kernel(
    q_ref, sk_ref, sv_ref, keys_ref, values_ref, slot_ref, len_ref, w_ref,
    out_ref,
    qmsg, qbuf, kbuf, vbuf, wbuf, bias, sbuf, smsg, rbuf, amsg, abuf, omsg, obuf,
    local_sem, part_send, part_recv, send_sem, recv_sem,
):
    pool = lax.axis_index("pool")
    tp = lax.axis_index("tp")
    core = lax.rem(pool, 2)
    chip = lax.div(pool, 2)
    x = lax.div(chip, NY)
    y = lax.rem(chip, NY)
    other = pool + 1 - 2 * core
    home = lax.div(x, NX // CONV)
    token = lax.rem(pool, SUF)

    def chip_at(step):
        to_x = lax.rem(x + far_first(NX, lax.rem(step, NX)), NX)
        to_y = lax.rem(y + far_first(NY, lax.div(step, NX)), NY)
        return to_x * NY + to_y

    local = [
        pltpu.make_async_copy(keys_ref, kbuf.at[pl.ds(0, PAIRS // 2)], local_sem.at[0]),
        pltpu.make_async_copy(values_ref, vbuf.at[pl.ds(0, PAIRS // 2)], local_sem.at[1]),
        pltpu.make_async_copy(w_ref, wbuf.at[core], local_sem.at[2]),
    ]
    for copy in local:
        copy.start()

    barrier = pltpu.get_barrier_semaphore()

    def greet(step, carry):
        to = chip_at(step)
        pl.semaphore_signal(barrier, inc=1, device_id=(to * 2 + core, tp), device_id_type=MESH)
        pl.semaphore_signal(barrier, inc=1, device_id=(to * 2 + 1 - core, tp), device_id_type=MESH)
        return carry

    lax.fori_loop(0, CHIPS - 1, greet, 0)

    def greet_tp(step, carry):
        to = lax.rem(tp + 1 + step, TP)
        pl.semaphore_signal(barrier, inc=1, device_id=(pool, to), device_id_type=MESH)
        pl.semaphore_signal(barrier, inc=1, device_id=(other, to), device_id_type=MESH)
        return carry

    lax.fori_loop(0, TP - 1, greet_tp, 0)
    pl.semaphore_signal(barrier, inc=1, device_id=(other, tp), device_id_type=MESH)

    rows = [q_ref[:, g * HD : (g + 1) * HD].astype(jnp.float32) for g in range(GROUPS)]
    rows += [sk_ref[...].astype(jnp.float32), sv_ref[...].astype(jnp.float32)]
    qmsg[...] = jnp.concatenate(rows, axis=0)

    slots = jnp.where(core == 0, slot_ref[0:1, :], slot_ref[1:2, :])
    pair = lax.broadcasted_iota(jnp.int32, (PAIRS, 1), 0)
    first = jnp.where(pair < PAIRS // 2, pool * PAIRS, other * PAIRS - PAIRS) + 2 * pair
    for side in range(2):
        found = jnp.max(jnp.where(slots == first + side, 1.0, 0.0), axis=1, keepdims=True)
        bias[:, side * HD : (side + 1) * HD] = jnp.broadcast_to(
            jnp.where(found > 0.5, 0.0, NEG), (PAIRS, HD)
        )

    pl.semaphore_wait(barrier, 2 * (CHIPS - 1) + 2 * (TP - 1) + 1)

    def send_queries(step, carry):
        to = chip_at(step) * 2 + home
        mine = qbuf.at[pl.ds(pl.multiple_of(token * 8, 8), 8)]

        @pl.when(to != pool)
        def _():
            pltpu.make_async_remote_copy(
                src_ref=qmsg, dst_ref=mine, send_sem=send_sem.at[0], recv_sem=recv_sem.at[0],
                device_id=(to, tp), device_id_type=MESH,
            ).start()

        @pl.when(to == pool)
        def _():
            pltpu.make_async_copy(qmsg, mine, recv_sem.at[0]).start()

        return carry

    lax.fori_loop(0, CHIPS, send_queries, 0)

    swaps = [
        pltpu.make_async_remote_copy(
            src_ref=src, dst_ref=dst, send_sem=part_send.at[n], recv_sem=part_recv.at[n],
            device_id=(other, tp), device_id_type=MESH,
        )
        for n, (src, dst) in enumerate(
            [
                (keys_ref, kbuf.at[pl.ds(PAIRS // 2, PAIRS // 2)]),
                (values_ref, vbuf.at[pl.ds(PAIRS // 2, PAIRS // 2)]),
                (w_ref, wbuf.at[core]),
            ]
        )
    ]
    for copy in swaps:
        copy.start()
    for copy in local:
        copy.wait()
    swaps[0].wait()
    swaps[1].wait()
    pltpu.make_async_copy(qbuf, qbuf, recv_sem.at[0]).wait()

    def head_rows(ref, row):
        return ref[pl.ds(row, SUF, stride=8), :]

    queries = jnp.concatenate([head_rows(qbuf, g) for g in range(GROUPS)], axis=0).astype(jnp.bfloat16)
    own_keys = head_rows(qbuf, 6).astype(jnp.bfloat16)
    own_values = head_rows(qbuf, 7).astype(jnp.bfloat16)
    contract = (((1,), (1,)), ((), ()))

    def score(r, top):
        s = lax.dot_general(queries, kbuf[r], contract, preferred_element_type=jnp.float32)
        s = s + bias[pl.ds(r, 1), :]
        sbuf[r] = s
        return jnp.maximum(top, jnp.maximum(s[:, :HD], s[:, HD:]))

    top = lax.fori_loop(0, PAIRS, score, jnp.full((ROWS, HD), NEG, jnp.float32), unroll=4)
    own = lax.dot_general(queries, own_keys, contract, preferred_element_type=jnp.float32)
    row_pos = lax.rem(lax.broadcasted_iota(jnp.int32, (ROWS, SUF), 0), SUF)
    key_pos = lax.broadcasted_iota(jnp.int32, (ROWS, SUF), 1)
    own = jnp.where((key_pos == chip) & (row_pos >= chip), own, NEG)
    row_max = jnp.maximum(
        jnp.max(top, axis=1, keepdims=True), jnp.max(own, axis=1, keepdims=True)
    )

    def add(r, carry):
        total, numer = carry
        p = jnp.exp2((sbuf[r] - row_max) * EXP_SCALE)
        total = total + (p[:, :HD] + p[:, HD:])
        numer = numer + jnp.dot(p.astype(jnp.bfloat16), vbuf[r], preferred_element_type=jnp.float32)
        return total, numer

    zero = jnp.zeros((ROWS, HD), jnp.float32)
    total, numer = lax.fori_loop(0, PAIRS, add, (zero, zero), unroll=4)
    p = jnp.exp2((own - row_max) * EXP_SCALE)
    numer = numer + jnp.dot(p.astype(jnp.bfloat16), own_values, preferred_element_type=jnp.float32)
    row_sum = jnp.sum(total, axis=1, keepdims=True) + jnp.sum(p, axis=1, keepdims=True)

    lane = lax.broadcasted_iota(jnp.int32, (SUF, HD), 1)
    maxima = jnp.zeros((SUF, HD), jnp.float32)
    sums = jnp.zeros((SUF, HD), jnp.float32)
    for g in range(GROUPS):
        part = slice(g * SUF, (g + 1) * SUF)
        smsg[pl.ds(g, SUF, stride=8), :] = numer[part]
        maxima = jnp.where(lane == g, row_max[part], maxima)
        sums = jnp.where(lane == g, row_sum[part], sums)
    smsg[pl.ds(6, SUF, stride=8), :] = maxima
    smsg[pl.ds(7, SUF, stride=8), :] = sums

    my_tile = pl.ds(pl.multiple_of(chip * 8, 8), 8)

    def send_state(step, carry):
        to = chip_at(step)
        pltpu.make_async_remote_copy(
            src_ref=smsg.at[pl.ds(pl.multiple_of(to * 8, 8), 8)], dst_ref=rbuf.at[my_tile],
            send_sem=send_sem.at[1], recv_sem=recv_sem.at[1],
            device_id=(to * 2 + core, tp), device_id_type=MESH,
        ).start()
        return carry

    lax.fori_loop(0, CHIPS - 1, send_state, 0)
    rbuf[my_tile, :] = smsg[my_tile, :]
    others = pl.ds(0, (CHIPS - 1) * 8)
    pltpu.make_async_copy(rbuf.at[others], rbuf.at[others], recv_sem.at[1]).wait()

    maxima = head_rows(rbuf, 6)
    sums = head_rows(rbuf, 7)
    best = jnp.max(maxima, axis=0, keepdims=True)
    scale = jnp.exp2((maxima - best) * EXP_SCALE)
    whole = jnp.sum(scale * sums, axis=0, keepdims=True)
    lane = lax.broadcasted_iota(jnp.int32, (1, HD), 1)
    scale = scale / jnp.where(lane < GROUPS, whole, 1.0)
    limit = jnp.where(core == 0, len_ref[:, 0:1], len_ref[:, 1:2])
    rows = []
    for g in range(GROUPS):
        row = jnp.sum(scale[:, g : g + 1] * head_rows(rbuf, g), axis=0, keepdims=True)
        rows.append(jnp.where(limit > chip, row, 0.0))
    rows.append(jnp.zeros((2, HD), jnp.float32))
    amsg[...] = jnp.concatenate(rows, axis=0)

    def send_attention(step, carry):
        to = chip_at(step)
        pltpu.make_async_remote_copy(
            src_ref=amsg, dst_ref=abuf.at[my_tile],
            send_sem=send_sem.at[2], recv_sem=recv_sem.at[2],
            device_id=(to * 2 + core, tp), device_id_type=MESH,
        ).start()
        return carry

    lax.fori_loop(0, CHIPS - 1, send_attention, 0)
    abuf[my_tile, :] = amsg[...]
    swaps[2].wait()
    pltpu.make_async_copy(abuf.at[others], abuf.at[others], recv_sem.at[2]).wait()

    attention = jnp.concatenate([head_rows(abuf, g) for g in range(GROUPS)], axis=1).astype(jnp.bfloat16)
    for side in range(2):
        share = jnp.dot(attention, wbuf[side], preferred_element_type=jnp.float32)
        for tile in range(TP // CONV):
            omsg[side, tile] = share[tile * 8 : (tile + 1) * 8]

    kept = core == lax.div(tp, TP // CONV)
    for side in range(2):
        for tile in range(TP // CONV):
            to = (chip * 2 + side, core * (TP // CONV) + tile)
            here = (to[0] == pool) & (to[1] == tp)

            @pl.when(jnp.logical_not(here))
            def _():
                pltpu.make_async_remote_copy(
                    src_ref=omsg.at[side, tile], dst_ref=obuf.at[tp],
                    send_sem=send_sem.at[3], recv_sem=recv_sem.at[3],
                    device_id=to, device_id_type=MESH,
                ).start()

            @pl.when(here)
            def _():
                pltpu.make_async_copy(omsg.at[side, tile], obuf.at[tp], recv_sem.at[3]).start()

    pltpu.make_async_copy(obuf, obuf, recv_sem.at[3]).wait()
    out_ref[...] = jnp.sum(obuf[...], axis=0).astype(out_ref.dtype)

    tiles = qbuf.at[others]
    for n in range(1, 3):
        pltpu.make_async_copy(tiles, tiles, send_sem.at[n]).wait()

    @pl.when(core == home)
    def _():
        pltpu.make_async_copy(tiles, tiles, send_sem.at[0]).wait()

    @pl.when(core != home)
    def _():
        pltpu.make_async_copy(qbuf, qbuf, send_sem.at[0]).wait()

    @pl.when(kept)
    def _():
        sent = obuf.at[pl.ds(0, TP - 1)]
        pltpu.make_async_copy(sent, sent, send_sem.at[3]).wait()

    @pl.when(jnp.logical_not(kept))
    def _():
        pltpu.make_async_copy(obuf, obuf, send_sem.at[3]).wait()


def shards(queries, suffix_keys, suffix_values, prefix_keys, prefix_values, block_slot, suffix_len, out_weight):
    f32, bf16 = jnp.float32, jnp.bfloat16
    columns = out_weight.shape[1]
    blocks = (PAIRS // 2, 2 * HD, HD)
    vmem = pl.BlockSpec(memory_space=pltpu.VMEM)
    anywhere = pl.BlockSpec(memory_space=pl.ANY)
    return pl.pallas_call(
        kernel,
        name="attend_and_project",
        out_shape=jax.ShapeDtypeStruct((8, columns), bf16),
        in_specs=[vmem, vmem, vmem, anywhere, anywhere, vmem, vmem, anywhere],
        out_specs=vmem,
        scratch_shapes=[
            pltpu.VMEM((8, HD), f32),
            pltpu.VMEM((SUF * 8, HD), f32),
            pltpu.VMEM((PAIRS, 2 * HD, HD), bf16),
            pltpu.VMEM((PAIRS, 2 * HD, HD), bf16),
            pltpu.VMEM((2, GROUPS * HD, columns), bf16),
            pltpu.VMEM((PAIRS, 2 * HD), f32),
            pltpu.VMEM((PAIRS, ROWS, 2 * HD), f32),
            pltpu.VMEM((SUF * 8, HD), f32),
            pltpu.VMEM((CHIPS * 8, HD), f32),
            pltpu.VMEM((8, HD), f32),
            pltpu.VMEM((CHIPS * 8, HD), f32),
            pltpu.VMEM((2, TP // CONV, 8, columns), f32),
            pltpu.VMEM((TP, 8, columns), f32),
            pltpu.SemaphoreType.DMA((3,)),
            pltpu.SemaphoreType.DMA((3,)),
            pltpu.SemaphoreType.DMA((3,)),
            pltpu.SemaphoreType.DMA((4,)),
            pltpu.SemaphoreType.DMA((4,)),
        ],
        compiler_params=pltpu.CompilerParams(
            collective_id=0, has_side_effects=True, vmem_limit_bytes=40 * 1024 * 1024
        ),
    )(
        queries,
        suffix_keys,
        suffix_values,
        prefix_keys.reshape(blocks),
        prefix_values.reshape(blocks),
        block_slot,
        suffix_len.reshape(1, CONV),
        out_weight,
    )


def solution(mesh):
    in_specs = (
        P("pool", "tp"),
        P("pool", "tp"),
        P("pool", "tp"),
        P("pool", None, "tp"),
        P("pool", None, "tp"),
        P(),
        P(),
        P("tp", "pool"),
    )
    return jax.shard_map(shards, mesh=mesh, in_specs=in_specs, out_specs=P("tp", "pool"), check_vma=False)
```

time: 335 us -> 46.9 us (0.14)
  the two profiles are of different devices: /device:TPU:2 before, /device:TPU:1 now
where the time goes in v1:
time: 46.9 us; the launch traced here: 46.7 us
  Pallas kernels  43.8 us (93%)
  local copies, waits for them, and re-layouts  2.84 us (6%)
    pallas_call x1, Pallas kernels, shards(): pl.pallas_call(kernel, name='attend_and_project', out_shape=jax.ShapeDtyp...  43.8 us
    unnamed x16, local copies, waits for them, and re-layouts  2.84 us

profile of v1, /device:TPU:1, one launch (start us, length us, event | category | flops | bytes accessed | tf_op | source)
XLA Modules:
  0.0 46.7 jit_solution(12489096698389612123)
XLA Ops:
  0.0 0.0 copy-start
  0.0 0.0 copy-start.2
  0.0 0.0 copy-start.3
  0.0 0.0 copy-start.4
  0.0 0.0 copy-start.5
  0.0 0.0 copy-start.6
  0.0 1.2 %copy.9.w_ref = bf16[768,192]{1,0:T(8,128)(2,1)S(1)} copy(bf16[768,192]{0,1:T(8,128)(2,1)} %param.15) | data formatting | bytes 589824 | tf_op args[7]
  1.2 0.0 copy-done
  1.2 0.0 copy-done.2
  1.2 0.0 copy-done.3
  1.3 0.0 copy-done.4
  1.3 0.0 copy-done.5
  1.3 0.0 copy-done.6
  1.3 0.0 copy-start.1
  1.3 1.0 %copy-done.1 = bf16[16,128,128]{2,1,0:T(8,128)(2,1)S(1)} copy-done((bf16[16,128,128]{2,1,0:T(8,128)(2,1)S(1)}, bf16[16,128,128]{2,1,0:T(8,128)(2,1)}, u32[]{:S(2)}) %copy-start.1) | copy-done | bytes 524312
  2.3 43.8 %attend_and_project.1 = bf16[8,192]{1,0:T(8,128)(2,1)S(1)} custom-call(bf16[1,768]{1,0:T(2,128)(2,1)S(1)} %copy-done.2, bf16[1,128]{1,0:T(2,128)(2,1)S(1)} %copy-done.4, bf16[1,128]{1,0:T(2,128)(2,1)S(1)} %copy-done.5, bf16[8,256,128]{2,1,0:T(8,128)(2,1)S(1)} %bitcast.3, bf16[8,256,128]{2,1,0:T(8,128)(2,1)S(1)} %bitcast.4, s32[2,256]{1,0:T(2,128)S(1)} %copy-done.3, ...), custom_call_target="tpu_custom_call" | custom-call | tf_op jit(solution)/shard_map/attend_and_project/pallas_call | solution.py:284
  46.1 0.6 %copy.11 = bf16[8,192]{1,0:T(8,128)(2,1)} copy(bf16[8,192]{1,0:T(8,128)(2,1)S(1)} %attend_and_project.1) | data formatting | bytes 6144
Async XLA Ops:
  0.0 1.2 %copy-start = (bf16[16,128,128]{2,1,0:T(8,128)(2,1)S(1)}, bf16[16,128,128]{2,1,0:T(8,128)(2,1)}, u32[]{:S(2)}) copy-start(bf16[16,128,128]{2,1,0:T(8,128)(2,1)} %param.11) | copy-start | bytes 1572868
  0.0 1.2 %copy-start.2 = (bf16[1,768]{1,0:T(2,128)(2,1)S(1)}, bf16[1,768]{1,0:T(2,128)(2,1)}, u32[]{:S(2)}) copy-start(bf16[1,768]{1,0:T(2,128)(2,1)} %q_ref.1) | copy-start | bytes 4612
  0.0 1.2 %copy-start.3 = (s32[2,256]{1,0:T(2,128)S(1)}, s32[2,256]{1,0:T(2,128)}, u32[]{:S(2)}) copy-start(s32[2,256]{1,0:T(2,128)} %slot_ref.1) | copy-start | bytes 6148
  0.0 1.2 %copy-start.4 = (bf16[1,128]{1,0:T(2,128)(2,1)S(1)}, bf16[1,128]{1,0:T(2,128)(2,1)}, u32[]{:S(2)}) copy-start(bf16[1,128]{1,0:T(2,128)(2,1)} %sk_ref.1) | copy-start | bytes 772
  0.0 1.2 %copy-start.5 = (bf16[1,128]{1,0:T(2,128)(2,1)S(1)}, bf16[1,128]{1,0:T(2,128)(2,1)}, u32[]{:S(2)}) copy-start(bf16[1,128]{1,0:T(2,128)(2,1)} %sv_ref.1) | copy-start | bytes 772
  0.0 1.2 %copy-start.6 = (s32[2]{0:T(128)S(1)}, s32[2]{0:T(128)}, u32[]{:S(2)}) copy-start(s32[2]{0:T(128)} %param.14) | copy-start | bytes 28
  1.3 1.0 %copy-start.1 = (bf16[16,128,128]{2,1,0:T(8,128)(2,1)S(1)}, bf16[16,128,128]{2,1,0:T(8,128)(2,1)}, u32[]{:S(2)}) copy-start(bf16[16,128,128]{2,1,0:T(8,128)(2,1)} %param.12) | copy-start | bytes 1572868

commit v2 on v1

v2 whole, which is shorter than its diff:
```python
import functools
import math

import jax
import jax.numpy as jnp
from jax import lax
from jax.experimental import pallas as pl
from jax.experimental.pallas import tpu as pltpu
from jax.sharding import PartitionSpec as P

H = 48
KVH = 8
HD = 128
CONV = 2
SUF = 32
GROUPS = H // KVH
NEG = -(2.0**100)
EXP_SCALE = math.log2(math.e) / math.sqrt(HD)
MESH = pl.DeviceIdType.MESH

NX = 4
NY = 8
CHIPS = NX * NY
TP = 8
PAIRS = 16
TILE = 8
TILES = SUF // TILE


def far_first(count, step):
    half = count // 2
    return half + (1 - 2 * (step % 2)) * ((step + 1) // 2)


NEARER = (
    (2, 1), (2, 7), (1, 2), (1, 6), (2, 0), (1, 1), (1, 7), (3, 1), (3, 7), (0, 2), (0, 6),
    (1, 0), (3, 0), (0, 1), (0, 7),
)


def opposite(chip):
    return (chip // NY + NX // 2) % NX * NY + (chip % NY + NY // 2) % NY


def couple(chip):
    across = chip // (CHIPS // 2)
    return chip - across * (CHIPS // 2) + across * ((chip % NY + NY // 2) % NY - chip % NY)


def kernel(
    q_hbm, sk_hbm, sv_hbm, keys_ref, values_ref, slot_hbm, len_hbm, w_ref,
    out_ref,
    q_ref, sk_ref, sv_ref, slot_ref, len_ref,
    qmsg, qbuf, kbuf, vbuf, wbuf, bias, sbuf, state, smsg, rbuf, merged, amsg, abuf, omsg, obuf,
    small_sem, local_sem, part_send, part_recv, query_sem, attend_sem, send_sem, recv_sem,
):
    pool = lax.axis_index("pool")
    tp = lax.axis_index("tp")
    core = lax.rem(pool, 2)
    chip = lax.div(pool, 2)
    x = lax.div(chip, NY)
    y = lax.rem(chip, NY)
    other = pool + 1 - 2 * core
    home = lax.div(x, NX // CONV)
    token = lax.rem(pool, SUF)

    row_of = [lax.rem(x + dx, NX) * NY for dx in range(NX)]
    place_of = [lax.rem(y + dy, NY) for dy in range(NY)]

    def chip_at(step):
        return row_of[far_first(NX, step % NX) % NX] + place_of[far_first(NY, step // NX) % NY]

    barrier = pltpu.get_barrier_semaphore()

    def greet(step, carry):
        to = chip_at(step)
        pl.semaphore_signal(barrier, inc=1, device_id=(to * 2 + core, tp), device_id_type=MESH)
        pl.semaphore_signal(barrier, inc=1, device_id=(to * 2 + 1 - core, tp), device_id_type=MESH)
        return carry

    for step in range(CHIPS - 1):
        greet(step, 0)

    def greet_tp(step, carry):
        to = lax.rem(tp + 1 + step, TP)
        pl.semaphore_signal(barrier, inc=1, device_id=(pool, to), device_id_type=MESH)
        pl.semaphore_signal(barrier, inc=1, device_id=(other, to), device_id_type=MESH)
        return carry

    for step in range(TP - 1):
        greet_tp(step, 0)
    pl.semaphore_signal(barrier, inc=1, device_id=(other, tp), device_id_type=MESH)

    small = [
        pltpu.make_async_copy(src, dst, small_sem.at[n])
        for n, (src, dst) in enumerate(
            [(q_hbm, q_ref), (sk_hbm, sk_ref), (sv_hbm, sv_ref), (slot_hbm, slot_ref), (len_hbm, len_ref)]
        )
    ]
    for copy in small:
        copy.start()
    local = [
        pltpu.make_async_copy(keys_ref, kbuf.at[pl.ds(0, PAIRS // 2)], local_sem.at[0]),
        pltpu.make_async_copy(values_ref, vbuf.at[pl.ds(0, PAIRS // 2)], local_sem.at[1]),
        pltpu.make_async_copy(w_ref, wbuf.at[core], local_sem.at[2]),
    ]
    for copy in local:
        copy.start()
    for copy in small:
        copy.wait()

    rows = [q_ref[:, g * HD : (g + 1) * HD].astype(jnp.float32) for g in range(GROUPS)]
    rows += [sk_ref[...].astype(jnp.float32), sv_ref[...].astype(jnp.float32)]
    qmsg[...] = jnp.concatenate(rows, axis=0)

    slots = jnp.where(core == 0, slot_ref[0:1, :], slot_ref[1:2, :])
    pair = lax.broadcasted_iota(jnp.int32, (PAIRS, 1), 0)
    first = jnp.where(pair < PAIRS // 2, pool * PAIRS, other * PAIRS - PAIRS) + 2 * pair
    for side in range(2):
        found = jnp.max(jnp.where(slots == first + side, 1.0, 0.0), axis=1, keepdims=True)
        bias[:, side * HD : (side + 1) * HD] = jnp.broadcast_to(
            jnp.where(found > 0.5, 0.0, NEG), (PAIRS, HD)
        )

    pl.semaphore_wait(barrier, 2 * (CHIPS - 1) + 2 * (TP - 1) + 1)

    for step in range(CHIPS):
        to = chip_at(step) * 2 + home
        mine = qbuf.at[pl.ds(pl.multiple_of(token * 8, 8), 8)]

        @pl.when(to != pool)
        def _():
            pltpu.make_async_remote_copy(
                src_ref=qmsg, dst_ref=mine, send_sem=send_sem.at[0], recv_sem=query_sem.at[token // TILE],
                device_id=(to, tp), device_id_type=MESH,
            ).start()

        @pl.when(to == pool)
        def _():
            pltpu.make_async_copy(qmsg, mine, query_sem.at[token // TILE]).start()

    swaps = [
        pltpu.make_async_remote_copy(
            src_ref=src, dst_ref=dst, send_sem=part_send.at[n], recv_sem=part_recv.at[n],
            device_id=(other, tp), device_id_type=MESH,
        )
        for n, (src, dst) in enumerate(
            [
                (keys_ref, kbuf.at[pl.ds(PAIRS // 2, PAIRS // 2)]),
                (values_ref, vbuf.at[pl.ds(PAIRS // 2, PAIRS // 2)]),
                (w_ref, wbuf.at[core]),
            ]
        )
    ]
    for copy in swaps:
        copy.start()
    for copy in local:
        copy.wait()
    swaps[0].wait()
    swaps[1].wait()

    contract = (((1,), (1,)), ((), ()))
    rows = GROUPS * TILE

    def wait_bytes(ref, sem):
        pltpu.make_async_copy(ref, ref, sem).wait()

    for tile in range(TILES):
        base = tile * TILE * 8
        here = pl.ds(base, TILE * 8)
        wait_bytes(qbuf.at[here], query_sem.at[tile])

        queries = jnp.concatenate(
            [qbuf[pl.ds(base + g, TILE, stride=8), :] for g in range(GROUPS)], axis=0
        ).astype(jnp.bfloat16)
        seen = TILE * (tile + 1)
        own_keys = qbuf[pl.ds(6, seen, stride=8), :].astype(jnp.bfloat16)
        own_values = qbuf[pl.ds(7, seen, stride=8), :].astype(jnp.bfloat16)
        top = jnp.full((rows, HD), NEG, jnp.float32)
        for r in range(PAIRS):
            s = lax.dot_general(queries, kbuf[r], contract, preferred_element_type=jnp.float32)
            s = s + bias[r : r + 1, :]
            sbuf[r] = s
            top = jnp.maximum(top, jnp.maximum(s[:, :HD], s[:, HD:]))
        own = lax.dot_general(queries, own_keys, contract, preferred_element_type=jnp.float32)
        row_pos = tile * TILE + lax.rem(lax.broadcasted_iota(jnp.int32, (rows, seen), 0), TILE)
        key_pos = lax.broadcasted_iota(jnp.int32, (rows, seen), 1)
        own = jnp.where((key_pos == chip) & (row_pos >= chip), own, NEG)
        row_max = jnp.maximum(
            jnp.max(top, axis=1, keepdims=True), jnp.max(own, axis=1, keepdims=True)
        )
        row_max = row_max.astype(jnp.bfloat16).astype(jnp.float32)

        p = jnp.exp2((own - row_max) * EXP_SCALE)
        row_sum = jnp.sum(p, axis=1, keepdims=True)
        numer = jnp.dot(p.astype(jnp.bfloat16), own_values, preferred_element_type=jnp.float32)
        total = jnp.zeros((rows, HD), jnp.float32)
        for r in range(PAIRS):
            p = jnp.exp2((sbuf[r] - row_max) * EXP_SCALE)
            total = total + (p[:, :HD] + p[:, HD:])
            numer = numer + jnp.dot(p.astype(jnp.bfloat16), vbuf[r], preferred_element_type=jnp.float32)
        row_sum = row_sum + jnp.sum(total, axis=1, keepdims=True)

        lane = lax.broadcasted_iota(jnp.int32, (TILE, HD), 1)
        rounded = row_sum.astype(jnp.bfloat16).astype(jnp.float32)
        left = row_sum - rounded
        maxima = jnp.zeros((TILE, HD), jnp.float32)
        sums = jnp.zeros((TILE, HD), jnp.float32)
        for g in range(GROUPS):
            part = slice(g * TILE, (g + 1) * TILE)
            state[pl.ds(base + g, TILE, stride=8), :] = numer[part]
            maxima = jnp.where(lane == g, row_max[part], maxima)
            sums = jnp.where(lane == g, rounded[part], sums)
            sums = jnp.where(lane == g + HD // 2, left[part], sums)
        state[pl.ds(base + 6, TILE, stride=8), :] = maxima
        state[pl.ds(base + 7, TILE, stride=8), :] = sums
        smsg[here, :] = state[here, :].astype(jnp.bfloat16)

        my_tile = rbuf.at[pl.ds(pl.multiple_of(chip * 16, 16), 16)]
        for u in range(tile * TILE // 2, (tile + 1) * TILE // 2):
            couple_rows = smsg.at[pl.ds(u * 16, 16)]
            for to in (u, opposite(u)):

                @pl.when(chip != to)
                def _():
                    pltpu.make_async_remote_copy(
                        src_ref=couple_rows, dst_ref=my_tile,
                        send_sem=send_sem.at[1], recv_sem=recv_sem.at[0],
                        device_id=(to * 2 + core, tp), device_id_type=MESH,
                    ).start()

                @pl.when(chip == to)
                def _():
                    pltpu.make_async_copy(couple_rows, my_tile, recv_sem.at[0]).start()

    wait_bytes(rbuf, recv_sem.at[0])
    merged[...] = rbuf[...].astype(jnp.float32)
    mine = couple(chip)
    lane = lax.broadcasted_iota(jnp.int32, (1, HD), 1)
    limit = jnp.where(core == 0, len_ref[:, 0:1], len_ref[:, 1:2])
    out_rows = []
    for half in range(2):

        def of_chips(row):
            return merged[pl.ds(half * 8 + row, CHIPS, stride=16), :]

        maxima = of_chips(6)
        sums = of_chips(7)
        sums = sums + pltpu.roll(sums, HD // 2, axis=1)
        best = jnp.max(maxima, axis=0, keepdims=True)
        scale = jnp.exp2((maxima - best) * EXP_SCALE)
        whole = jnp.sum(scale * sums, axis=0, keepdims=True)
        scale = scale / jnp.where(lane < GROUPS, whole, 1.0)
        for g in range(GROUPS):
            row = jnp.sum(scale[:, g : g + 1] * of_chips(g), axis=0, keepdims=True)
            out_rows.append(jnp.where(limit > 2 * mine + half, row, 0.0))
        out_rows.append(jnp.zeros((2, HD), jnp.float32))
    amsg[...] = jnp.concatenate(out_rows, axis=0).astype(jnp.bfloat16)

    my_couple = abuf.at[pl.ds(pl.multiple_of(mine * 16, 16), 16)]
    arrived = attend_sem.at[mine // (TILE // 2)]
    for dx, dy in NEARER:
        to = row_of[dx] + place_of[dy]
        pltpu.make_async_remote_copy(
            src_ref=amsg, dst_ref=my_couple, send_sem=send_sem.at[2], recv_sem=arrived,
            device_id=(to * 2 + core, tp), device_id_type=MESH,
        ).start()
    pltpu.make_async_copy(amsg, my_couple, arrived).start()
    swaps[2].wait()

    my_share = obuf.at[tp]
    for tile in range(TILES):
        here = pl.ds(tile * TILE * 8, TILE * 8)
        wait_bytes(abuf.at[here], attend_sem.at[tile])
        state[here, :] = abuf[here, :].astype(jnp.float32)
        attention = jnp.concatenate(
            [state[pl.ds(tile * TILE * 8 + g, TILE, stride=8), :] for g in range(GROUPS)], axis=1
        ).astype(jnp.bfloat16)
        for side in (1, 0):
            share = lax.dot_general(attention, wbuf[side], contract, preferred_element_type=jnp.float32)
            rest = jnp.concatenate(
                [share[:, HD:], jnp.zeros((TILE, 2 * HD - share.shape[1]), jnp.float32)], axis=1
            )
            omsg[side, tile] = jnp.concatenate([share[:, :HD], rest], axis=0).astype(jnp.bfloat16)
            to = (chip * 2 + side, core * TILES + tile)
            stays = (to[0] == pool) & (to[1] == tp)

            @pl.when(jnp.logical_not(stays))
            def _():
                pltpu.make_async_remote_copy(
                    src_ref=omsg.at[side, tile], dst_ref=my_share,
                    send_sem=send_sem.at[3], recv_sem=recv_sem.at[1],
                    device_id=to, device_id_type=MESH,
                ).start()

            @pl.when(stays)
            def _():
                pltpu.make_async_copy(omsg.at[side, tile], my_share, recv_sem.at[1]).start()

    wait_bytes(obuf, recv_sem.at[1])
    result = jnp.sum(obuf[...].astype(jnp.float32), axis=0)
    out_ref[:, :HD] = result[:TILE].astype(out_ref.dtype)
    out_ref[:, HD:] = result[TILE:, : out_ref.shape[1] - HD].astype(out_ref.dtype)

    wait_bytes(rbuf.at[pl.ds(0, (CHIPS - 1) * 16)], send_sem.at[1])
    wait_bytes(abuf.at[pl.ds(0, len(NEARER) * 16)], send_sem.at[2])

    @pl.when(core == home)
    def _():
        wait_bytes(qbuf.at[pl.ds(0, (CHIPS - 1) * 8)], send_sem.at[0])

    @pl.when(core != home)
    def _():
        wait_bytes(qbuf, send_sem.at[0])

    @pl.when(core == tp // TILES)
    def _():
        wait_bytes(obuf.at[pl.ds(0, TP - 1)], send_sem.at[3])

    @pl.when(core != tp // TILES)
    def _():
        wait_bytes(obuf, send_sem.at[3])


def shards(queries, suffix_keys, suffix_values, prefix_keys, prefix_values, block_slot, suffix_len, out_weight):
    f32, bf16 = jnp.float32, jnp.bfloat16
    columns = out_weight.shape[1]
    blocks = (PAIRS // 2, 2 * HD, HD)
    in_hbm = pl.BlockSpec(memory_space=pl.ANY)
    return pl.pallas_call(
        kernel,
        name="attend_and_project",
        out_shape=jax.ShapeDtypeStruct((8, columns), bf16),
        in_specs=[in_hbm] * 8,
        out_specs=pl.BlockSpec(memory_space=pltpu.VMEM),
        scratch_shapes=[
            pltpu.VMEM(queries.shape, bf16),
            pltpu.VMEM(suffix_keys.shape, bf16),
            pltpu.VMEM(suffix_values.shape, bf16),
            pltpu.VMEM(block_slot.shape, jnp.int32),
            pltpu.VMEM((1, CONV), jnp.int32),
            pltpu.VMEM((8, HD), f32),
            pltpu.VMEM((SUF * 8, HD), f32),
            pltpu.VMEM((PAIRS, 2 * HD, HD), bf16),
            pltpu.VMEM((PAIRS, 2 * HD, HD), bf16),
            pltpu.VMEM((2, columns, GROUPS * HD), bf16),
            pltpu.VMEM((PAIRS, 2 * HD), f32),
            pltpu.VMEM((PAIRS, GROUPS * TILE, 2 * HD), f32),
            pltpu.VMEM((SUF * 8, HD), f32),
            pltpu.VMEM((SUF * 8, HD), bf16),
            pltpu.VMEM((CHIPS * 16, HD), bf16),
            pltpu.VMEM((CHIPS * 16, HD), f32),
            pltpu.VMEM((16, HD), bf16),
            pltpu.VMEM((SUF * 8, HD), bf16),
            pltpu.VMEM((2, TILES, 2 * TILE, HD), bf16),
            pltpu.VMEM((TP, 2 * TILE, HD), bf16),
            pltpu.SemaphoreType.DMA((5,)),
            pltpu.SemaphoreType.DMA((3,)),
            pltpu.SemaphoreType.DMA((3,)),
            pltpu.SemaphoreType.DMA((3,)),
            pltpu.SemaphoreType.DMA((TILES,)),
            pltpu.SemaphoreType.DMA((TILES,)),
            pltpu.SemaphoreType.DMA((4,)),
            pltpu.SemaphoreType.DMA((2,)),
        ],
        compiler_params=pltpu.CompilerParams(
            collective_id=0, has_side_effects=True, vmem_limit_bytes=56 * 1024 * 1024
        ),
    )(
        queries,
        suffix_keys,
        suffix_values,
        prefix_keys.reshape(blocks),
        prefix_values.reshape(blocks),
        block_slot,
        suffix_len.reshape(1, CONV),
        out_weight.T,
    )


def solution(mesh):
    in_specs = (
        P("pool", "tp"),
        P("pool", "tp"),
        P("pool", "tp"),
        P("pool", None, "tp"),
        P("pool", None, "tp"),
        P(),
        P(),
        P("tp", "pool"),
    )
    return jax.shard_map(shards, mesh=mesh, in_specs=in_specs, out_specs=P("tp", "pool"), check_vma=False)
```

time: 46.9 us -> 40.5 us (0.86)
  Pallas kernels: 43.8 us -> 39.1 us
  local copies, waits for them, and re-layouts: 2.84 us -> 1.28 us
    pallas_call x1, Pallas kernels: 43.8 us -> 39.1 us  [shards(): pl.pallas_call(kernel, name='attend_and_project', out_shape=jax.ShapeDtyp...]
    unnamed x16 -> x1, local copies, waits for them, and re-layouts: 2.84 us -> 1.28 us
where the time goes in v2:
time: 40.5 us; the launch traced here: 40.4 us
  Pallas kernels  39.1 us (97%)
  local copies, waits for them, and re-layouts  1.28 us (3%)
    pallas_call x1, Pallas kernels, shards(): pl.pallas_call(kernel, name='attend_and_project', out_shape=jax.ShapeDtyp...  39.1 us
    unnamed x1, local copies, waits for them, and re-layouts  1.28 us

profile of v2, /device:TPU:1, one launch (start us, length us, event | category | flops | bytes accessed | tf_op | source)
XLA Modules:
  0.0 40.4 jit_solution(18218758228936877890)
XLA Ops:
  0.0 39.1 %attend_and_project.1 = bf16[8,192]{1,0:T(8,128)(2,1)} custom-call(bf16[1,768]{1,0:T(2,128)(2,1)} %q_hbm.1, bf16[1,128]{1,0:T(2,128)(2,1)} %sk_hbm.1, bf16[1,128]{1,0:T(2,128)(2,1)} %sv_hbm.1, bf16[8,256,128]{2,1,0:T(8,128)(2,1)} %bitcast.4, bf16[8,256,128]{2,1,0:T(8,128)(2,1)} %bitcast.5, s32[2,256]{1,0:T(2,128)} %slot_hbm.1, s32[1,2]{1,0:T(1,128)} %bitcast.7, ...), custom_call_target="tpu_custom_call" | custom-call | tf_op jit(solution)/shard_map/attend_and_project/pallas_call | solution.py:330
  39.1 1.3 %copy.10 = bf16[8,192]{1,0:T(8,128)(2,1)} copy(bf16[8,192]{1,0:T(8,128)(2,1)} %attend_and_project.1) | data formatting | bytes 6144

commit v3 on v2

v3 whole, which is shorter than its diff:
```python
import functools
import math

import jax
import jax.numpy as jnp
from jax import lax
from jax.experimental import pallas as pl
from jax.experimental.pallas import tpu as pltpu
from jax.sharding import PartitionSpec as P

H = 48
KVH = 8
HD = 128
CONV = 2
SUF = 32
GROUPS = H // KVH
NEG = -(2.0**100)
EXP_SCALE = math.log2(math.e) / math.sqrt(HD)
MESH = pl.DeviceIdType.MESH

NX = 4
NY = 8
CHIPS = NX * NY
TP = 8
PAIRS = 16
TILE = 8
TILES = SUF // TILE
GROUPED = ((0,), (1,), (2, 3))


def far_first(count, step):
    half = count // 2
    return half + (1 - 2 * (step % 2)) * ((step + 1) // 2)


CLASSES = 8
NEARER = ((2, 0), (1, 1), (1, 7), (1, 0), (3, 0), (0, 1), (0, 7))


def class_of(chip):
    return chip // NY % 2 * 4 + (chip % NY + 2 * (chip // (CHIPS // 2))) % 4


def owners(which):
    return [chip for chip in range(CHIPS) if class_of(chip) == which]


def kernel(
    q_hbm, sk_hbm, sv_hbm, keys_ref, values_ref, slot_hbm, len_hbm, w_ref,
    out_ref,
    q_ref, sk_ref, sv_ref, slot_ref, len_ref,
    qmsg, pmsg, qbuf, kbuf, vbuf, wbuf, bias, sbuf, state, smsg, rbuf, merged, amsg, abuf, omsg, obuf,
    small_sem, local_sem, part_send, part_recv, query_sem, attend_sem, send_sem, recv_sem, ready_sem,
):
    pool = lax.axis_index("pool")
    tp = lax.axis_index("tp")
    core = lax.rem(pool, 2)
    chip = lax.div(pool, 2)
    x = lax.div(chip, NY)
    y = lax.rem(chip, NY)
    other = pool + 1 - 2 * core
    home = lax.div(y, NY // 2)
    token = x * TILE + lax.rem(y, NY // 2) * 2 + core

    row_of = [lax.rem(x + dx, NX) * NY for dx in range(NX)]
    place_of = [lax.rem(y + dy, NY) for dy in range(NY)]

    def chip_at(step):
        return row_of[far_first(NX, step % NX) % NX] + place_of[far_first(NY, step // NX) % NY]

    barrier = pltpu.get_barrier_semaphore()

    def greet(step, carry):
        to = chip_at(step)
        pl.semaphore_signal(barrier, inc=1, device_id=(to * 2 + core, tp), device_id_type=MESH)
        pl.semaphore_signal(barrier, inc=1, device_id=(to * 2 + 1 - core, tp), device_id_type=MESH)
        return carry

    for step in range(CHIPS - 1):
        greet(step, 0)

    for step in range(1, TP):

        @pl.when(tp + step < TP)
        def _():
            for to in (pool, other):
                pl.semaphore_signal(barrier, inc=1, device_id=(to, tp + step), device_id_type=MESH)

    pl.semaphore_signal(barrier, inc=1, device_id=(other, tp), device_id_type=MESH)

    small = [
        pltpu.make_async_copy(src, dst, small_sem.at[n])
        for n, (src, dst) in enumerate(
            [(q_hbm, q_ref), (sk_hbm, sk_ref), (sv_hbm, sv_ref), (slot_hbm, slot_ref), (len_hbm, len_ref)]
        )
    ]
    for copy in small:
        copy.start()
    local = [
        pltpu.make_async_copy(keys_ref, kbuf.at[pl.ds(0, PAIRS // 2)], local_sem.at[0]),
        pltpu.make_async_copy(values_ref, vbuf.at[pl.ds(0, PAIRS // 2)], local_sem.at[1]),
        pltpu.make_async_copy(w_ref, wbuf.at[core], local_sem.at[2]),
    ]
    for copy in local:
        copy.start()
    for copy in small:
        copy.wait()

    rows = [q_ref[:, g * HD : (g + 1) * HD].astype(jnp.float32) for g in range(GROUPS)]
    rows += [sk_ref[...].astype(jnp.float32), sv_ref[...].astype(jnp.float32)]
    qmsg[...] = jnp.concatenate(rows, axis=0)

    pair = lax.broadcasted_iota(jnp.int32, (PAIRS, 1), 0)
    first = jnp.where(pair < PAIRS // 2, pool * PAIRS, other * PAIRS - PAIRS) + 2 * pair
    for conv in range(CONV):
        for side in range(2):
            found = jnp.max(
                jnp.where(slot_ref[conv : conv + 1, :] == first + side, 1.0, 0.0), axis=1, keepdims=True
            )
            bias[conv, :, side * HD : (side + 1) * HD] = jnp.broadcast_to(
                jnp.where(found > 0.5, 0.0, NEG), (PAIRS, HD)
            )

    pl.semaphore_wait(barrier, 2 * (CHIPS - 1) + 1 + 2 * tp)

    for step in range(CHIPS):
        to = chip_at(step) * 2 + home
        mine = qbuf.at[pl.ds(pl.multiple_of(token * 8, 8), 8)]

        @pl.when(to != pool)
        def _():
            pltpu.make_async_remote_copy(
                src_ref=qmsg, dst_ref=mine, send_sem=send_sem.at[0], recv_sem=query_sem.at[token // TILE],
                device_id=(to, tp), device_id_type=MESH,
            ).start()

        @pl.when(to == pool)
        def _():
            pltpu.make_async_copy(qmsg, mine, query_sem.at[token // TILE]).start()

    for step in range(1, TP):

        @pl.when(tp - step >= 0)
        def _():
            for to in (pool, other):
                pl.semaphore_signal(ready_sem, inc=1, device_id=(to, tp - step), device_id_type=MESH)

    swaps = [
        pltpu.make_async_remote_copy(
            src_ref=src, dst_ref=dst, send_sem=part_send.at[n], recv_sem=part_recv.at[n],
            device_id=(other, tp), device_id_type=MESH,
        )
        for n, (src, dst) in enumerate(
            [
                (keys_ref, kbuf.at[pl.ds(PAIRS // 2, PAIRS // 2)]),
                (values_ref, vbuf.at[pl.ds(PAIRS // 2, PAIRS // 2)]),
                (w_ref, wbuf.at[core]),
                (qmsg, pmsg),
            ]
        )
    ]
    for copy in swaps[3:] + swaps[:3]:
        copy.start()
    for copy in local:
        copy.wait()
    for n in (3, 0, 1):
        swaps[n].wait()

    contract = (((1,), (1,)), ((), ()))

    def wait_bytes(ref, sem):
        pltpu.make_async_copy(ref, ref, sem).wait()

    tiles = (qmsg[...], pmsg[...])
    tiles = (jnp.where(core == 0, tiles[0], tiles[1]), jnp.where(core == 0, tiles[1], tiles[0]))
    blank = jnp.zeros((6, HD), jnp.float32)
    own_keys, own_values = [
        jnp.concatenate([tiles[0][row : row + 1], tiles[1][row : row + 1], blank], axis=0).astype(jnp.bfloat16)
        for row in (6, 7)
    ]
    own_pos = lax.rem(x, 2) * (SUF // 2) + 2 * y

    for group in GROUPED:
        conv = group[0] // (TILES // CONV)
        tokens = TILE * len(group)
        rows = GROUPS * tokens
        base = group[0] * TILE * 8
        here = pl.ds(base, tokens * 8)
        for tile in group:
            wait_bytes(qbuf.at[pl.ds(tile * TILE * 8, TILE * 8)], query_sem.at[tile])

        queries = jnp.concatenate(
            [qbuf[pl.ds(base + g, tokens, stride=8), :] for g in range(GROUPS)], axis=0
        ).astype(jnp.bfloat16)
        top = jnp.full((rows, HD), NEG, jnp.float32)
        for r in range(PAIRS):
            s = lax.dot_general(queries, kbuf[r], contract, preferred_element_type=jnp.float32)
            s = s + bias[conv, r : r + 1, :]
            sbuf[r, 0:rows] = s
            top = jnp.maximum(top, jnp.maximum(s[:, :HD], s[:, HD:]))
        own = lax.dot_general(queries, own_keys, contract, preferred_element_type=jnp.float32)
        at = lax.rem(lax.broadcasted_iota(jnp.int32, (rows, 8), 0), tokens) + group[0] % 2 * TILE
        row_pos = (at // TILE * 2 + core) * TILE + at % TILE
        key = lax.broadcasted_iota(jnp.int32, (rows, 8), 1)
        own = jnp.where((key < 2) & (row_pos >= own_pos + key) & (x // 2 == conv), own, NEG)
        row_max = jnp.maximum(
            jnp.max(top, axis=1, keepdims=True), jnp.max(own, axis=1, keepdims=True)
        )
        row_max = row_max.astype(jnp.bfloat16).astype(jnp.float32)

        p = jnp.exp2((own - row_max) * EXP_SCALE)
        row_sum = jnp.sum(p, axis=1, keepdims=True)
        numer = jnp.dot(p.astype(jnp.bfloat16), own_values, preferred_element_type=jnp.float32)
        total = jnp.zeros((rows, HD), jnp.float32)
        for r in range(PAIRS):
            p = jnp.exp2((sbuf[r, 0:rows] - row_max) * EXP_SCALE)
            total = total + (p[:, :HD] + p[:, HD:])
            numer = numer + jnp.dot(p.astype(jnp.bfloat16), vbuf[r], preferred_element_type=jnp.float32)
        row_sum = row_sum + jnp.sum(total, axis=1, keepdims=True)

        lane = lax.broadcasted_iota(jnp.int32, (tokens, HD), 1)
        rounded = row_sum.astype(jnp.bfloat16).astype(jnp.float32)
        left = row_sum - rounded
        maxima = jnp.zeros((tokens, HD), jnp.float32)
        sums = jnp.zeros((tokens, HD), jnp.float32)
        for g in range(GROUPS):
            part = slice(g * tokens, (g + 1) * tokens)
            state[pl.ds(base + g, tokens, stride=8), :] = numer[part]
            maxima = jnp.where(lane == g, row_max[part], maxima)
            sums = jnp.where(lane == g, rounded[part], sums)
            sums = jnp.where(lane == g + HD // 2, left[part], sums)
        state[pl.ds(base + 6, tokens, stride=8), :] = maxima
        state[pl.ds(base + 7, tokens, stride=8), :] = sums
        smsg[here, :] = state[here, :].astype(jnp.bfloat16)

        my_tile = rbuf.at[conv, pl.ds(pl.multiple_of(chip * 16, 16), 16)]
        for couple in range(group[0] * TILE // 2, (group[-1] + 1) * TILE // 2):
            couple_rows = smsg.at[pl.ds(couple * 16, 16)]
            for to in owners(couple % CLASSES):

                @pl.when(chip != to)
                def _():
                    pltpu.make_async_remote_copy(
                        src_ref=couple_rows, dst_ref=my_tile,
                        send_sem=send_sem.at[1], recv_sem=recv_sem.at[conv],
                        device_id=(to * 2 + core, tp), device_id_type=MESH,
                    ).start()

                @pl.when(chip == to)
                def _():
                    pltpu.make_async_copy(couple_rows, my_tile, recv_sem.at[conv]).start()

    mine = class_of(chip)

    def merge(conv):
        wait_bytes(rbuf.at[conv], recv_sem.at[conv])
        merged[...] = rbuf[conv].astype(jnp.float32)
        lane = lax.broadcasted_iota(jnp.int32, (1, HD), 1)
        limit = len_ref[:, conv : conv + 1]
        out_rows = []
        for half in range(2):

            def of_chips(row):
                return merged[pl.ds(half * 8 + row, CHIPS, stride=16), :]

            maxima = of_chips(6)
            sums = of_chips(7)
            sums = sums + pltpu.roll(sums, HD // 2, axis=1)
            best = jnp.max(maxima, axis=0, keepdims=True)
            scale = jnp.exp2((maxima - best) * EXP_SCALE)
            whole = jnp.sum(scale * sums, axis=0, keepdims=True)
            scale = scale / jnp.where(lane < GROUPS, whole, 1.0)
            position = (mine // 4 * 2 + core) * TILE + mine % 4 * 2 + half
            for g in range(GROUPS):
                row = jnp.sum(scale[:, g : g + 1] * of_chips(g), axis=0, keepdims=True)
                out_rows.append(jnp.where(limit > position, row, 0.0))
            out_rows.append(jnp.zeros((2, HD), jnp.float32))
        amsg[conv] = jnp.concatenate(out_rows, axis=0).astype(jnp.bfloat16)

        my_couple = abuf.at[pl.ds(pl.multiple_of((conv * CLASSES + mine) * 16, 16), 16)]
        arrived = attend_sem.at[conv * 2 + mine // 4]
        for dx, dy in NEARER:
            to = row_of[dx] + place_of[dy]
            pltpu.make_async_remote_copy(
                src_ref=amsg.at[conv], dst_ref=my_couple, send_sem=send_sem.at[2], recv_sem=arrived,
                device_id=(to * 2 + core, tp), device_id_type=MESH,
            ).start()
        pltpu.make_async_copy(amsg.at[conv], my_couple, arrived).start()

    my_share = obuf.at[tp]

    def project(tile):
        here = pl.ds(tile * TILE * 8, TILE * 8)
        wait_bytes(abuf.at[here], attend_sem.at[tile])
        state[here, :] = abuf[here, :].astype(jnp.float32)
        attention = jnp.concatenate(
            [state[pl.ds(tile * TILE * 8 + g, TILE, stride=8), :] for g in range(GROUPS)], axis=1
        ).astype(jnp.bfloat16)
        for side in (1, 0):
            share = lax.dot_general(attention, wbuf[side], contract, preferred_element_type=jnp.float32)
            rest = jnp.concatenate(
                [share[:, HD:], jnp.zeros((TILE, 2 * HD - share.shape[1]), jnp.float32)], axis=1
            )
            omsg[side, tile] = jnp.concatenate([share[:, :HD], rest], axis=0).astype(jnp.bfloat16)
            to = (chip * 2 + side, 2 * tile + core)
            stays = (to[0] == pool) & (to[1] == tp)

            @pl.when(jnp.logical_not(stays))
            def _():
                pltpu.make_async_remote_copy(
                    src_ref=omsg.at[side, tile], dst_ref=my_share,
                    send_sem=send_sem.at[3], recv_sem=recv_sem.at[2],
                    device_id=to, device_id_type=MESH,
                ).start()

            @pl.when(stays)
            def _():
                pltpu.make_async_copy(omsg.at[side, tile], my_share, recv_sem.at[2]).start()

    merge(0)
    swaps[2].wait()

    @pl.when(tp < TP - 1)
    def _():
        pl.semaphore_wait(ready_sem, 2 * (TP - 1 - tp))

    project(0)
    project(1)
    merge(1)
    project(2)
    project(3)

    wait_bytes(obuf, recv_sem.at[2])
    result = jnp.sum(obuf[...].astype(jnp.float32), axis=0)
    out_ref[:, :HD] = result[:TILE].astype(out_ref.dtype)
    out_ref[:, HD:] = result[TILE:, : out_ref.shape[1] - HD].astype(out_ref.dtype)

    for conv in range(CONV):
        wait_bytes(rbuf.at[conv, pl.ds(0, (CHIPS - 1) * 16)], send_sem.at[1])
        wait_bytes(abuf.at[pl.ds(0, len(NEARER) * 16)], send_sem.at[2])

    @pl.when(core == home)
    def _():
        wait_bytes(qbuf.at[pl.ds(0, (CHIPS - 1) * 8)], send_sem.at[0])

    @pl.when(core != home)
    def _():
        wait_bytes(qbuf, send_sem.at[0])

    @pl.when(core == tp % 2)
    def _():
        wait_bytes(obuf.at[pl.ds(0, TP - 1)], send_sem.at[3])

    @pl.when(core != tp % 2)
    def _():
        wait_bytes(obuf, send_sem.at[3])


def shards(queries, suffix_keys, suffix_values, prefix_keys, prefix_values, block_slot, suffix_len, out_weight):
    f32, bf16 = jnp.float32, jnp.bfloat16
    columns = out_weight.shape[1]
    blocks = (PAIRS // 2, 2 * HD, HD)
    in_hbm = pl.BlockSpec(memory_space=pl.ANY)
    return pl.pallas_call(
        kernel,
        name="attend_and_project",
        out_shape=jax.ShapeDtypeStruct((8, columns), bf16),
        in_specs=[in_hbm] * 8,
        out_specs=pl.BlockSpec(memory_space=pltpu.VMEM),
        scratch_shapes=[
            pltpu.VMEM(queries.shape, bf16),
            pltpu.VMEM(suffix_keys.shape, bf16),
            pltpu.VMEM(suffix_values.shape, bf16),
            pltpu.VMEM(block_slot.shape, jnp.int32),
            pltpu.VMEM((1, CONV), jnp.int32),
            pltpu.VMEM((8, HD), f32),
            pltpu.VMEM((8, HD), f32),
            pltpu.VMEM((SUF * 8, HD), f32),
            pltpu.VMEM((PAIRS, 2 * HD, HD), bf16),
            pltpu.VMEM((PAIRS, 2 * HD, HD), bf16),
            pltpu.VMEM((2, columns, GROUPS * HD), bf16),
            pltpu.VMEM((CONV, PAIRS, 2 * HD), f32),
            pltpu.VMEM((PAIRS, GROUPS * TILE * max(map(len, GROUPED)), 2 * HD), f32),
            pltpu.VMEM((SUF * 8, HD), f32),
            pltpu.VMEM((SUF * 8, HD), bf16),
            pltpu.VMEM((CONV, CHIPS * 16, HD), bf16),
            pltpu.VMEM((CHIPS * 16, HD), f32),
            pltpu.VMEM((CONV, 16, HD), bf16),
            pltpu.VMEM((SUF * 8, HD), bf16),
            pltpu.VMEM((2, TILES, 2 * TILE, HD), bf16),
            pltpu.VMEM((TP, 2 * TILE, HD), bf16),
            pltpu.SemaphoreType.DMA((5,)),
            pltpu.SemaphoreType.DMA((3,)),
            pltpu.SemaphoreType.DMA((4,)),
            pltpu.SemaphoreType.DMA((4,)),
            pltpu.SemaphoreType.DMA((TILES,)),
            pltpu.SemaphoreType.DMA((TILES,)),
            pltpu.SemaphoreType.DMA((4,)),
            pltpu.SemaphoreType.DMA((3,)),
            pltpu.SemaphoreType.REGULAR,
        ],
        compiler_params=pltpu.CompilerParams(
            collective_id=0, has_side_effects=True, vmem_limit_bytes=56 * 1024 * 1024
        ),
    )(
        queries,
        suffix_keys,
        suffix_values,
        prefix_keys.reshape(blocks),
        prefix_values.reshape(blocks),
        block_slot,
        suffix_len.reshape(1, CONV),
        out_weight.T,
    )


def solution(mesh):
    in_specs = (
        P("pool", "tp"),
        P("pool", "tp"),
        P("pool", "tp"),
        P("pool", None, "tp"),
        P("pool", None, "tp"),
        P(),
        P(),
        P("tp", "pool"),
    )
    return jax.shard_map(shards, mesh=mesh, in_specs=in_specs, out_specs=P("tp", "pool"), check_vma=False)
```

time: 40.5 us -> 40.2 us (level)
  no operation moved by 1% of the time
where the time goes in v3:
time: 40.2 us; the launch traced here: 40 us
  Pallas kernels  38.7 us (96%)
  local copies, waits for them, and re-layouts  1.28 us (3%)
    pallas_call x1, Pallas kernels, shards(): pl.pallas_call(kernel, name='attend_and_project', out_shape=jax.ShapeDtyp...  38.7 us
    unnamed x1, local copies, waits for them, and re-layouts  1.28 us

profile of v3, /device:TPU:1, one launch (start us, length us, event | category | flops | bytes accessed | tf_op | source)
XLA Modules:
  0.0 40.0 jit_solution(10018367623407183842)
XLA Ops:
  0.0 38.7 %attend_and_project.1 = bf16[8,192]{1,0:T(8,128)(2,1)} custom-call(bf16[1,768]{1,0:T(2,128)(2,1)} %q_hbm.1, bf16[1,128]{1,0:T(2,128)(2,1)} %sk_hbm.1, bf16[1,128]{1,0:T(2,128)(2,1)} %sv_hbm.1, bf16[8,256,128]{2,1,0:T(8,128)(2,1)} %bitcast.4, bf16[8,256,128]{2,1,0:T(8,128)(2,1)} %bitcast.5, s32[2,256]{1,0:T(2,128)} %slot_hbm.1, s32[1,2]{1,0:T(1,128)} %bitcast.7, ...), custom_call_target="tpu_custom_call" | custom-call | tf_op jit(solution)/shard_map/attend_and_project/pallas_call | solution.py:364
  38.8 1.3 %copy.10 = bf16[8,192]{1,0:T(8,128)(2,1)} copy(bf16[8,192]{1,0:T(8,128)(2,1)} %attend_and_project.1) | data formatting | bytes 6144

commit v4 on v3

--- a/solution.py
+++ b/solution.py
@@ -43,6 +43,13 @@
 
 def owners(which):
     return [chip for chip in range(CHIPS) if class_of(chip) == which]
+
+
+LAST_X, LAST_Y = 2, 4
+
+
+def hops_to_last(chip):
+    return abs(chip // NY - LAST_X) + abs(chip % NY - LAST_Y)
 
 
 def kernel(
@@ -108,7 +115,7 @@
 
     rows = [q_ref[:, g * HD : (g + 1) * HD].astype(jnp.float32) for g in range(GROUPS)]
     rows += [sk_ref[...].astype(jnp.float32), sv_ref[...].astype(jnp.float32)]
-    qmsg[...] = jnp.concatenate(rows, axis=0)
+    qmsg[...] = jnp.concatenate(rows, axis=0).astype(jnp.bfloat16)
 
     pair = lax.broadcasted_iota(jnp.int32, (PAIRS, 1), 0)
     first = jnp.where(pair < PAIRS // 2, pool * PAIRS, other * PAIRS - PAIRS) + 2 * pair
@@ -125,7 +132,7 @@
 
     for step in range(CHIPS):
         to = chip_at(step) * 2 + home
-        mine = qbuf.at[pl.ds(pl.multiple_of(token * 8, 8), 8)]
+        mine = qbuf.at[token]
 
         @pl.when(to != pool)
         def _():
@@ -171,7 +178,7 @@
     def wait_bytes(ref, sem):
         pltpu.make_async_copy(ref, ref, sem).wait()
 
-    tiles = (qmsg[...], pmsg[...])
+    tiles = (qmsg[...].astype(jnp.float32), pmsg[...].astype(jnp.float32))
     tiles = (jnp.where(core == 0, tiles[0], tiles[1]), jnp.where(core == 0, tiles[1], tiles[0]))
     blank = jnp.zeros((6, HD), jnp.float32)
     own_keys, own_values = [
@@ -187,10 +194,11 @@
         base = group[0] * TILE * 8
         here = pl.ds(base, tokens * 8)
         for tile in group:
-            wait_bytes(qbuf.at[pl.ds(tile * TILE * 8, TILE * 8)], query_sem.at[tile])
-
+            wait_bytes(qbuf.at[pl.ds(tile * TILE, TILE)], query_sem.at[tile])
+
+        state[here, :] = qbuf[group[0] * TILE : group[0] * TILE + tokens].astype(jnp.float32).reshape(tokens * 8, HD)
         queries = jnp.concatenate(
-            [qbuf[pl.ds(base + g, tokens, stride=8), :] for g in range(GROUPS)], axis=0
+            [state[pl.ds(base + g, tokens, stride=8), :] for g in range(GROUPS)], axis=0
         ).astype(jnp.bfloat16)
         top = jnp.full((rows, HD), NEG, jnp.float32)
         for r in range(PAIRS):
@@ -234,21 +242,25 @@
         smsg[here, :] = state[here, :].astype(jnp.bfloat16)
 
         my_tile = rbuf.at[conv, pl.ds(pl.multiple_of(chip * 16, 16), 16)]
-        for couple in range(group[0] * TILE // 2, (group[-1] + 1) * TILE // 2):
+        targets = [
+            (to, couple)
+            for couple in range(group[0] * TILE // 2, (group[-1] + 1) * TILE // 2)
+            for to in owners(couple % CLASSES)
+        ]
+        for to, couple in sorted(targets, key=lambda target: -hops_to_last(target[0])):
             couple_rows = smsg.at[pl.ds(couple * 16, 16)]
-            for to in owners(couple % CLASSES):
-
-                @pl.when(chip != to)
-                def _():
-                    pltpu.make_async_remote_copy(
-                        src_ref=couple_rows, dst_ref=my_tile,
-                        send_sem=send_sem.at[1], recv_sem=recv_sem.at[conv],
-                        device_id=(to * 2 + core, tp), device_id_type=MESH,
-                    ).start()
-
-                @pl.when(chip == to)
-                def _():
-                    pltpu.make_async_copy(couple_rows, my_tile, recv_sem.at[conv]).start()
+
+            @pl.when(chip != to)
+            def _():
+                pltpu.make_async_remote_copy(
+                    src_ref=couple_rows, dst_ref=my_tile,
+                    send_sem=send_sem.at[1], recv_sem=recv_sem.at[conv],
+                    device_id=(to * 2 + core, tp), device_id_type=MESH,
+                ).start()
+
+            @pl.when(chip == to)
+            def _():
+                pltpu.make_async_copy(couple_rows, my_tile, recv_sem.at[conv]).start()
 
     mine = class_of(chip)
 
@@ -325,8 +337,8 @@
         pl.semaphore_wait(ready_sem, 2 * (TP - 1 - tp))
 
     project(0)
+    merge(1)
     project(1)
-    merge(1)
     project(2)
     project(3)
 
@@ -341,7 +353,7 @@
 
     @pl.when(core == home)
     def _():
-        wait_bytes(qbuf.at[pl.ds(0, (CHIPS - 1) * 8)], send_sem.at[0])
+        wait_bytes(qbuf.at[pl.ds(0, CHIPS - 1)], send_sem.at[0])
 
     @pl.when(core != home)
     def _():
@@ -373,9 +385,9 @@
             pltpu.VMEM(suffix_values.shape, bf16),
             pltpu.VMEM(block_slot.shape, jnp.int32),
             pltpu.VMEM((1, CONV), jnp.int32),
-            pltpu.VMEM((8, HD), f32),
-            pltpu.VMEM((8, HD), f32),
-            pltpu.VMEM((SUF * 8, HD), f32),
+            pltpu.VMEM((8, HD), bf16),
+            pltpu.VMEM((8, HD), bf16),
+            pltpu.VMEM((SUF, 8, HD), bf16),
             pltpu.VMEM((PAIRS, 2 * HD, HD), bf16),
             pltpu.VMEM((PAIRS, 2 * HD, HD), bf16),
             pltpu.VMEM((2, columns, GROUPS * HD), bf16),
@@ -400,7 +412,7 @@
             pltpu.SemaphoreType.REGULAR,
         ],
         compiler_params=pltpu.CompilerParams(
-            collective_id=0, has_side_effects=True, vmem_limit_bytes=56 * 1024 * 1024
+            collective_id=0, has_side_effects=True, vmem_limit_bytes=55040 * 1024
         ),
     )(
         queries,

time: 40.2 us -> 38.9 us (0.968)
  Pallas kernels: 38.7 us -> 37.4 us
    pallas_call x1, Pallas kernels: 38.7 us -> 37.4 us  [shards(): pl.pallas_call(kernel, name='attend_and_project', out_shape=jax.ShapeDtyp...]
    unnamed x1 -> x11, local copies, waits for them, and re-layouts: 1.28 us -> 1.3 us
where the time goes in v4:
time: 38.9 us; the launch traced here: 38.7 us
  Pallas kernels  37.4 us (96%)
  local copies, waits for them, and re-layouts  1.3 us (3%)
    pallas_call x1, Pallas kernels, shards(): pl.pallas_call(kernel, name='attend_and_project', out_shape=jax.ShapeDtyp...  37.4 us
    unnamed x11, local copies, waits for them, and re-layouts  1.3 us

profile of v4, /device:TPU:1, one launch (start us, length us, event | category | flops | bytes accessed | tf_op | source)
XLA Modules:
  0.0 38.7 jit_solution(505896661220329008)
XLA Ops:
  0.0 0.0 copy-start.3
  0.0 0.0 copy-start.4
  0.0 0.0 copy-start
  0.0 0.0 copy-start.1
  0.0 0.0 copy-start.2
  0.0 0.6 %copy-done.3 = bf16[1,128]{1,0:T(2,128)(2,1)S(1)} copy-done((bf16[1,128]{1,0:T(2,128)(2,1)S(1)}, bf16[1,128]{1,0:T(2,128)(2,1)}, u32[]{:S(2)}) %copy-start.3) | copy-done | bytes 280
  0.7 0.0 copy-done.4
  0.7 0.0 copy-done
  0.7 0.0 copy-done.1
  0.7 0.0 copy-done.2
  0.7 37.4 %attend_and_project.1 = bf16[8,192]{1,0:T(8,128)(2,1)S(1)} custom-call(bf16[1,768]{1,0:T(2,128)(2,1)S(1)} %copy-done, bf16[1,128]{1,0:T(2,128)(2,1)S(1)} %copy-done.2, bf16[1,128]{1,0:T(2,128)(2,1)S(1)} %copy-done.3, bf16[8,256,128]{2,1,0:T(8,128)(2,1)} %bitcast.5, bf16[8,256,128]{2,1,0:T(8,128)(2,1)} %bitcast.6, s32[2,256]{1,0:T(2,128)S(1)} %copy-done.1, ...), custom_call_target="tpu_custom_call" | custom-call | tf_op jit(solution)/shard_map/attend_and_project/pallas_call | solution.py:376
  38.1 0.6 %copy.10 = bf16[8,192]{1,0:T(8,128)(2,1)} copy(bf16[8,192]{1,0:T(8,128)(2,1)S(1)} %attend_and_project.1) | data formatting | bytes 6144
Async XLA Ops:
  0.0 0.7 %copy-start.3 = (bf16[1,128]{1,0:T(2,128)(2,1)S(1)}, bf16[1,128]{1,0:T(2,128)(2,1)}, u32[]{:S(2)}) copy-start(bf16[1,128]{1,0:T(2,128)(2,1)} %sv_hbm.1) | copy-start | bytes 772
  0.0 0.7 %copy-start.4 = (s32[2]{0:T(128)S(1)}, s32[2]{0:T(128)}, u32[]{:S(2)}) copy-start(s32[2]{0:T(128)} %param.14) | copy-start | bytes 28
  0.0 0.7 %copy-start = (bf16[1,768]{1,0:T(2,128)(2,1)S(1)}, bf16[1,768]{1,0:T(2,128)(2,1)}, u32[]{:S(2)}) copy-start(bf16[1,768]{1,0:T(2,128)(2,1)} %q_hbm.1) | copy-start | bytes 4612
  0.0 0.7 %copy-start.1 = (s32[2,256]{1,0:T(2,128)S(1)}, s32[2,256]{1,0:T(2,128)}, u32[]{:S(2)}) copy-start(s32[2,256]{1,0:T(2,128)} %slot_hbm.1) | copy-start | bytes 6148
  0.0 0.7 %copy-start.2 = (bf16[1,128]{1,0:T(2,128)(2,1)S(1)}, bf16[1,128]{1,0:T(2,128)(2,1)}, u32[]{:S(2)}) copy-start(bf16[1,128]{1,0:T(2,128)(2,1)} %sk_hbm.1) | copy-start | bytes 772

commit v5 on v4

--- a/solution.py
+++ b/solution.py
@@ -34,15 +34,21 @@
 
 
 CLASSES = 8
-NEARER = ((2, 0), (1, 1), (1, 7), (1, 0), (3, 0), (0, 1), (0, 7))
+NEARER = (
+    ((2, 0), (1, 1), (1, 7), (1, 0), (3, 0), (0, 1), (0, 7)),
+    (
+        (2, 2), (3, 2), (1, 2), (2, 7), (2, 1), (0, 2), (3, 7), (3, 1),
+        (2, 0), (1, 1), (1, 7), (1, 0), (3, 0), (0, 1), (0, 7),
+    ),
+)
 
 
 def class_of(chip):
     return chip // NY % 2 * 4 + (chip % NY + 2 * (chip // (CHIPS // 2))) % 4
 
 
-def owners(which):
-    return [chip for chip in range(CHIPS) if class_of(chip) == which]
+def owners(which, conv):
+    return [chip for chip in range(CHIPS // (1 + conv)) if class_of(chip) == which]
 
 
 LAST_X, LAST_Y = 2, 4
@@ -56,8 +62,8 @@
     q_hbm, sk_hbm, sv_hbm, keys_ref, values_ref, slot_hbm, len_hbm, w_ref,
     out_ref,
     q_ref, sk_ref, sv_ref, slot_ref, len_ref,
-    qmsg, pmsg, qbuf, kbuf, vbuf, wbuf, bias, sbuf, state, smsg, rbuf, merged, amsg, abuf, omsg, obuf,
-    small_sem, local_sem, part_send, part_recv, query_sem, attend_sem, send_sem, recv_sem, ready_sem,
+    qmsg, pmsg, qbuf, kbuf, vbuf, wbuf, bias, sbuf, state, smsg, rbuf, fbuf, merged, amsg, abuf, omsg, obuf,
+    small_sem, local_sem, part_send, part_recv, query_sem, attend_sem, send_sem, recv_sem, first_sem, ready_sem,
 ):
     pool = lax.axis_index("pool")
     tp = lax.axis_index("tp")
@@ -245,7 +251,7 @@
         targets = [
             (to, couple)
             for couple in range(group[0] * TILE // 2, (group[-1] + 1) * TILE // 2)
-            for to in owners(couple % CLASSES)
+            for to in owners(couple % CLASSES, conv)
         ]
         for to, couple in sorted(targets, key=lambda target: -hops_to_last(target[0])):
             couple_rows = smsg.at[pl.ds(couple * 16, 16)]
@@ -254,7 +260,7 @@
             def _():
                 pltpu.make_async_remote_copy(
                     src_ref=couple_rows, dst_ref=my_tile,
-                    send_sem=send_sem.at[1], recv_sem=recv_sem.at[conv],
+                    send_sem=send_sem.at[1 + 4 * conv], recv_sem=recv_sem.at[conv],
                     device_id=(to * 2 + core, tp), device_id_type=MESH,
                 ).start()
 
@@ -262,11 +268,23 @@
             def _():
                 pltpu.make_async_copy(couple_rows, my_tile, recv_sem.at[conv]).start()
 
+        if group == (0,):
+            part = smsg.at[pl.ds(16, 48)]
+
+            @pl.when((core == 0) & (chip != 0))
+            def _():
+                pltpu.make_async_remote_copy(
+                    src_ref=part, dst_ref=fbuf.at[chip], send_sem=first_sem.at[0], recv_sem=first_sem.at[1],
+                    device_id=(0, tp), device_id_type=MESH,
+                ).start()
+
+            @pl.when(pool == 0)
+            def _():
+                pltpu.make_async_copy(part, fbuf.at[0], first_sem.at[1]).start()
+
     mine = class_of(chip)
 
-    def merge(conv):
-        wait_bytes(rbuf.at[conv], recv_sem.at[conv])
-        merged[...] = rbuf[conv].astype(jnp.float32)
+    def merge_couple(merged, which, conv):
         lane = lax.broadcasted_iota(jnp.int32, (1, HD), 1)
         limit = len_ref[:, conv : conv + 1]
         out_rows = []
@@ -282,19 +300,24 @@
             scale = jnp.exp2((maxima - best) * EXP_SCALE)
             whole = jnp.sum(scale * sums, axis=0, keepdims=True)
             scale = scale / jnp.where(lane < GROUPS, whole, 1.0)
-            position = (mine // 4 * 2 + core) * TILE + mine % 4 * 2 + half
+            position = (which // 4 * 2 + core) * TILE + which % 4 * 2 + half
             for g in range(GROUPS):
                 row = jnp.sum(scale[:, g : g + 1] * of_chips(g), axis=0, keepdims=True)
                 out_rows.append(jnp.where(limit > position, row, 0.0))
             out_rows.append(jnp.zeros((2, HD), jnp.float32))
-        amsg[conv] = jnp.concatenate(out_rows, axis=0).astype(jnp.bfloat16)
+        return jnp.concatenate(out_rows, axis=0).astype(jnp.bfloat16)
+
+    def merge(conv):
+        wait_bytes(rbuf.at[conv], recv_sem.at[conv])
+        merged[0] = rbuf[conv].astype(jnp.float32)
+        amsg[conv] = merge_couple(merged.at[0], mine, conv)
 
         my_couple = abuf.at[pl.ds(pl.multiple_of((conv * CLASSES + mine) * 16, 16), 16)]
         arrived = attend_sem.at[conv * 2 + mine // 4]
-        for dx, dy in NEARER:
+        for dx, dy in NEARER[conv]:
             to = row_of[dx] + place_of[dy]
             pltpu.make_async_remote_copy(
-                src_ref=amsg.at[conv], dst_ref=my_couple, send_sem=send_sem.at[2], recv_sem=arrived,
+                src_ref=amsg.at[conv], dst_ref=my_couple, send_sem=send_sem.at[2 + 2 * conv], recv_sem=arrived,
                 device_id=(to * 2 + core, tp), device_id_type=MESH,
             ).start()
         pltpu.make_async_copy(amsg.at[conv], my_couple, arrived).start()
@@ -303,8 +326,27 @@
 
     def project(tile):
         here = pl.ds(tile * TILE * 8, TILE * 8)
-        wait_bytes(abuf.at[here], attend_sem.at[tile])
-        state[here, :] = abuf[here, :].astype(jnp.float32)
+
+        def arrived():
+            wait_bytes(abuf.at[here], attend_sem.at[tile])
+            state[here, :] = abuf[here, :].astype(jnp.float32)
+
+        if tile == 0:
+            pl.when(pool != 0)(arrived)
+
+            @pl.when(pool == 0)
+            def _():
+                wait_bytes(fbuf, first_sem.at[1])
+                state[0:16, :] = amsg[0].astype(jnp.float32)
+                for which in range(1, 4):
+                    states = fbuf[:, (which - 1) * 16 : which * 16, :]
+                    merged[which] = states.astype(jnp.float32).reshape(CHIPS * 16, HD)
+                for which in range(1, 4):
+                    couple_rows = merge_couple(merged.at[which], which, 0)
+                    state[which * 16 : (which + 1) * 16, :] = couple_rows.astype(jnp.float32)
+
+        else:
+            arrived()
         attention = jnp.concatenate(
             [state[pl.ds(tile * TILE * 8 + g, TILE, stride=8), :] for g in range(GROUPS)], axis=1
         ).astype(jnp.bfloat16)
@@ -337,7 +379,7 @@
         pl.semaphore_wait(ready_sem, 2 * (TP - 1 - tp))
 
     project(0)
-    merge(1)
+    pl.when(x < NX // 2)(lambda: merge(1))
     project(1)
     project(2)
     project(3)
@@ -347,9 +389,25 @@
     out_ref[:, :HD] = result[:TILE].astype(out_ref.dtype)
     out_ref[:, HD:] = result[TILE:, : out_ref.shape[1] - HD].astype(out_ref.dtype)
 
-    for conv in range(CONV):
-        wait_bytes(rbuf.at[conv, pl.ds(0, (CHIPS - 1) * 16)], send_sem.at[1])
-        wait_bytes(abuf.at[pl.ds(0, len(NEARER) * 16)], send_sem.at[2])
+    @pl.when((core == 0) & (chip != 0))
+    def _():
+        wait_bytes(fbuf.at[0], first_sem.at[0])
+
+    @pl.when(pool == 0)
+    def _():
+        wait_bytes(abuf.at[pl.ds(0, TILE * 8)], attend_sem.at[0])
+
+    wait_bytes(rbuf.at[0, pl.ds(0, (CHIPS - 1) * 16)], send_sem.at[1])
+    wait_bytes(abuf.at[pl.ds(0, len(NEARER[0]) * 16)], send_sem.at[2])
+
+    @pl.when(x < NX // 2)
+    def _():
+        wait_bytes(rbuf.at[1, pl.ds(0, (CHIPS // 2 - 1) * 16)], send_sem.at[5])
+        wait_bytes(abuf.at[pl.ds(0, len(NEARER[1]) * 16)], send_sem.at[4])
+
+    @pl.when(x >= NX // 2)
+    def _():
+        wait_bytes(rbuf.at[1, pl.ds(0, CHIPS // 2 * 16)], send_sem.at[5])
 
     @pl.when(core == home)
     def _():
@@ -396,7 +454,8 @@
             pltpu.VMEM((SUF * 8, HD), f32),
             pltpu.VMEM((SUF * 8, HD), bf16),
             pltpu.VMEM((CONV, CHIPS * 16, HD), bf16),
-            pltpu.VMEM((CHIPS * 16, HD), f32),
+            pltpu.VMEM((CHIPS, 48, HD), bf16),
+            pltpu.VMEM((4, CHIPS * 16, HD), f32),
             pltpu.VMEM((CONV, 16, HD), bf16),
             pltpu.VMEM((SUF * 8, HD), bf16),
             pltpu.VMEM((2, TILES, 2 * TILE, HD), bf16),
@@ -407,8 +466,9 @@
             pltpu.SemaphoreType.DMA((4,)),
             pltpu.SemaphoreType.DMA((TILES,)),
             pltpu.SemaphoreType.DMA((TILES,)),
-            pltpu.SemaphoreType.DMA((4,)),
+            pltpu.SemaphoreType.DMA((6,)),
             pltpu.SemaphoreType.DMA((3,)),
+            pltpu.SemaphoreType.DMA((2,)),
             pltpu.SemaphoreType.REGULAR,
         ],
         compiler_params=pltpu.CompilerParams(

time: 38.9 us -> 38 us (0.977); the launches traced: 38.7 us -> 37.4 us
  Pallas kernels: 37.4 us -> 36.1 us
    pallas_call x1, Pallas kernels: 37.4 us -> 36.1 us  [shards(): pl.pallas_call(kernel, name='attend_and_project', out_shape=jax.ShapeDtyp...]
where the time goes in v5:
time: 38 us; the launch traced here: 37.4 us
  Pallas kernels  36.1 us (95%)
  local copies, waits for them, and re-layouts  1.3 us (3%)
    pallas_call x1, Pallas kernels, shards(): pl.pallas_call(kernel, name='attend_and_project', out_shape=jax.ShapeDtyp...  36.1 us
    unnamed x11, local copies, waits for them, and re-layouts  1.3 us

profile of v5, /device:TPU:1, one launch (start us, length us, event | category | flops | bytes accessed | tf_op | source)
XLA Modules:
  0.0 37.4 jit_solution(17533961789327222162)
XLA Ops:
  0.0 0.0 copy-start.3
  0.0 0.0 copy-start.4
  0.0 0.0 copy-start
  0.0 0.0 copy-start.1
  0.0 0.0 copy-start.2
  0.0 0.6 %copy-done.3 = bf16[1,128]{1,0:T(2,128)(2,1)S(1)} copy-done((bf16[1,128]{1,0:T(2,128)(2,1)S(1)}, bf16[1,128]{1,0:T(2,128)(2,1)}, u32[]{:S(2)}) %copy-start.3) | copy-done | bytes 280
  0.7 0.0 copy-done.4
  0.7 0.0 copy-done
  0.7 0.0 copy-done.1
  0.7 0.0 copy-done.2
  0.7 36.1 %attend_and_project.1 = bf16[8,192]{1,0:T(8,128)(2,1)S(1)} custom-call(bf16[1,768]{1,0:T(2,128)(2,1)S(1)} %copy-done, bf16[1,128]{1,0:T(2,128)(2,1)S(1)} %copy-done.2, bf16[1,128]{1,0:T(2,128)(2,1)S(1)} %copy-done.3, bf16[8,256,128]{2,1,0:T(8,128)(2,1)} %bitcast.5, bf16[8,256,128]{2,1,0:T(8,128)(2,1)} %bitcast.6, s32[2,256]{1,0:T(2,128)S(1)} %copy-done.1, ...), custom_call_target="tpu_custom_call" | custom-call | tf_op jit(solution)/shard_map/attend_and_project/pallas_call | solution.py:434
  36.8 0.6 %copy.10 = bf16[8,192]{1,0:T(8,128)(2,1)} copy(bf16[8,192]{1,0:T(8,128)(2,1)S(1)} %attend_and_project.1) | data formatting | bytes 6144
Async XLA Ops:
  0.0 0.7 %copy-start.3 = (bf16[1,128]{1,0:T(2,128)(2,1)S(1)}, bf16[1,128]{1,0:T(2,128)(2,1)}, u32[]{:S(2)}) copy-start(bf16[1,128]{1,0:T(2,128)(2,1)} %sv_hbm.1) | copy-start | bytes 772
  0.0 0.7 %copy-start.4 = (s32[2]{0:T(128)S(1)}, s32[2]{0:T(128)}, u32[]{:S(2)}) copy-start(s32[2]{0:T(128)} %param.14) | copy-start | bytes 28
  0.0 0.7 %copy-start = (bf16[1,768]{1,0:T(2,128)(2,1)S(1)}, bf16[1,768]{1,0:T(2,128)(2,1)}, u32[]{:S(2)}) copy-start(bf16[1,768]{1,0:T(2,128)(2,1)} %q_hbm.1) | copy-start | bytes 4612
  0.0 0.7 %copy-start.1 = (s32[2,256]{1,0:T(2,128)S(1)}, s32[2,256]{1,0:T(2,128)}, u32[]{:S(2)}) copy-start(s32[2,256]{1,0:T(2,128)} %slot_hbm.1) | copy-start | bytes 6148
  0.0 0.7 %copy-start.2 = (bf16[1,128]{1,0:T(2,128)(2,1)S(1)}, bf16[1,128]{1,0:T(2,128)(2,1)}, u32[]{:S(2)}) copy-start(bf16[1,128]{1,0:T(2,128)(2,1)} %sk_hbm.1) | copy-start | bytes 772

commit v6 on v5

--- a/solution.py
+++ b/solution.py
@@ -25,7 +25,7 @@
 PAIRS = 16
 TILE = 8
 TILES = SUF // TILE
-GROUPED = ((0,), (1,), (2, 3))
+GROUPED = ((0,), (1,), (2,), (3,))
 
 
 def far_first(count, step):

time: 38 us -> 37.7 us (level)
  Pallas kernels: 36.1 us -> 35.6 us
    pallas_call x1, Pallas kernels: 36.1 us -> 35.6 us  [shards(): pl.pallas_call(kernel, name='attend_and_project', out_shape=jax.ShapeDtyp...]
where the time goes in v6:
time: 37.7 us; the launch traced here: 37 us
  Pallas kernels  35.6 us (94%)
  local copies, waits for them, and re-layouts  1.3 us (3%)
    pallas_call x1, Pallas kernels, shards(): pl.pallas_call(kernel, name='attend_and_project', out_shape=jax.ShapeDtyp...  35.6 us
    unnamed x11, local copies, waits for them, and re-layouts  1.3 us

profile of v6, /device:TPU:1, one launch (start us, length us, event | category | flops | bytes accessed | tf_op | source)
XLA Modules:
  0.0 37.0 jit_solution(2048842809281911635)
XLA Ops:
  0.0 0.0 copy-start.3
  0.0 0.0 copy-start.4
  0.0 0.0 copy-start
  0.0 0.0 copy-start.1
  0.0 0.0 copy-start.2
  0.0 0.6 %copy-done.3 = bf16[1,128]{1,0:T(2,128)(2,1)S(1)} copy-done((bf16[1,128]{1,0:T(2,128)(2,1)S(1)}, bf16[1,128]{1,0:T(2,128)(2,1)}, u32[]{:S(2)}) %copy-start.3) | copy-done | bytes 280
  0.7 0.0 copy-done.4
  0.7 0.0 copy-done
  0.7 0.0 copy-done.1
  0.7 0.0 copy-done.2
  0.7 35.6 %attend_and_project.1 = bf16[8,192]{1,0:T(8,128)(2,1)S(1)} custom-call(bf16[1,768]{1,0:T(2,128)(2,1)S(1)} %copy-done, bf16[1,128]{1,0:T(2,128)(2,1)S(1)} %copy-done.2, bf16[1,128]{1,0:T(2,128)(2,1)S(1)} %copy-done.3, bf16[8,256,128]{2,1,0:T(8,128)(2,1)} %bitcast.5, bf16[8,256,128]{2,1,0:T(8,128)(2,1)} %bitcast.6, s32[2,256]{1,0:T(2,128)S(1)} %copy-done.1, ...), custom_call_target="tpu_custom_call" | custom-call | tf_op jit(solution)/shard_map/attend_and_project/pallas_call | solution.py:434
  36.4 0.6 %copy.10 = bf16[8,192]{1,0:T(8,128)(2,1)} copy(bf16[8,192]{1,0:T(8,128)(2,1)S(1)} %attend_and_project.1) | data formatting | bytes 6144
Async XLA Ops:
  0.0 0.7 %copy-start.3 = (bf16[1,128]{1,0:T(2,128)(2,1)S(1)}, bf16[1,128]{1,0:T(2,128)(2,1)}, u32[]{:S(2)}) copy-start(bf16[1,128]{1,0:T(2,128)(2,1)} %sv_hbm.1) | copy-start | bytes 772
  0.0 0.7 %copy-start.4 = (s32[2]{0:T(128)S(1)}, s32[2]{0:T(128)}, u32[]{:S(2)}) copy-start(s32[2]{0:T(128)} %param.14) | copy-start | bytes 28
  0.0 0.7 %copy-start = (bf16[1,768]{1,0:T(2,128)(2,1)S(1)}, bf16[1,768]{1,0:T(2,128)(2,1)}, u32[]{:S(2)}) copy-start(bf16[1,768]{1,0:T(2,128)(2,1)} %q_hbm.1) | copy-start | bytes 4612
  0.0 0.7 %copy-start.1 = (s32[2,256]{1,0:T(2,128)S(1)}, s32[2,256]{1,0:T(2,128)}, u32[]{:S(2)}) copy-start(s32[2,256]{1,0:T(2,128)} %slot_hbm.1) | copy-start | bytes 6148
  0.0 0.7 %copy-start.2 = (bf16[1,128]{1,0:T(2,128)(2,1)S(1)}, bf16[1,128]{1,0:T(2,128)(2,1)}, u32[]{:S(2)}) copy-start(bf16[1,128]{1,0:T(2,128)(2,1)} %sk_hbm.1) | copy-start | bytes 772

commit v7 on v6

--- a/solution.py
+++ b/solution.py
@@ -193,6 +193,8 @@
     ]
     own_pos = lax.rem(x, 2) * (SUF // 2) + 2 * y
 
+    mine = class_of(chip)
+
     for group in GROUPED:
         conv = group[0] // (TILES // CONV)
         tokens = TILE * len(group)
@@ -254,19 +256,19 @@
             for to in owners(couple % CLASSES, conv)
         ]
         for to, couple in sorted(targets, key=lambda target: -hops_to_last(target[0])):
-            couple_rows = smsg.at[pl.ds(couple * 16, 16)]
 
             @pl.when(chip != to)
             def _():
                 pltpu.make_async_remote_copy(
-                    src_ref=couple_rows, dst_ref=my_tile,
+                    src_ref=smsg.at[pl.ds(couple * 16, 16)], dst_ref=my_tile,
                     send_sem=send_sem.at[1 + 4 * conv], recv_sem=recv_sem.at[conv],
                     device_id=(to * 2 + core, tp), device_id_type=MESH,
                 ).start()
 
-            @pl.when(chip == to)
-            def _():
-                pltpu.make_async_copy(couple_rows, my_tile, recv_sem.at[conv]).start()
+        @pl.when((mine // 4 == group[0] % 2) & (x < NX // (1 + conv)))
+        def _():
+            own_rows = smsg.at[pl.ds(pl.multiple_of((conv * CLASSES + mine) * 16, 16), 16)]
+            pltpu.make_async_copy(own_rows, my_tile, recv_sem.at[conv]).start()
 
         if group == (0,):
             part = smsg.at[pl.ds(16, 48)]
@@ -281,8 +283,6 @@
             @pl.when(pool == 0)
             def _():
                 pltpu.make_async_copy(part, fbuf.at[0], first_sem.at[1]).start()
-
-    mine = class_of(chip)
 
     def merge_couple(merged, which, conv):
         lane = lax.broadcasted_iota(jnp.int32, (1, HD), 1)
@@ -309,7 +309,7 @@
 
     def merge(conv):
         wait_bytes(rbuf.at[conv], recv_sem.at[conv])
-        merged[0] = rbuf[conv].astype(jnp.float32)
+        merged[0, 0 : CHIPS * 16] = rbuf[conv].astype(jnp.float32)
         amsg[conv] = merge_couple(merged.at[0], mine, conv)
 
         my_couple = abuf.at[pl.ds(pl.multiple_of((conv * CLASSES + mine) * 16, 16), 16)]
@@ -340,7 +340,7 @@
                 state[0:16, :] = amsg[0].astype(jnp.float32)
                 for which in range(1, 4):
                     states = fbuf[:, (which - 1) * 16 : which * 16, :]
-                    merged[which] = states.astype(jnp.float32).reshape(CHIPS * 16, HD)
+                    merged[which, 0 : CHIPS * 16] = states.astype(jnp.float32).reshape(CHIPS * 16, HD)
                 for which in range(1, 4):
                     couple_rows = merge_couple(merged.at[which], which, 0)
                     state[which * 16 : (which + 1) * 16, :] = couple_rows.astype(jnp.float32)
@@ -451,11 +451,11 @@
             pltpu.VMEM((2, columns, GROUPS * HD), bf16),
             pltpu.VMEM((CONV, PAIRS, 2 * HD), f32),
             pltpu.VMEM((PAIRS, GROUPS * TILE * max(map(len, GROUPED)), 2 * HD), f32),
-            pltpu.VMEM((SUF * 8, HD), f32),
+            pltpu.VMEM((SUF * 8 + 8, HD), f32),
             pltpu.VMEM((SUF * 8, HD), bf16),
             pltpu.VMEM((CONV, CHIPS * 16, HD), bf16),
             pltpu.VMEM((CHIPS, 48, HD), bf16),
-            pltpu.VMEM((4, CHIPS * 16, HD), f32),
+            pltpu.VMEM((4, CHIPS * 16 + 16, HD), f32),
             pltpu.VMEM((CONV, 16, HD), bf16),
             pltpu.VMEM((SUF * 8, HD), bf16),
             pltpu.VMEM((2, TILES, 2 * TILE, HD), bf16),

time: 37.7 us -> 37.6 us (level)
  no operation moved by 1% of the time
where the time goes in v7:
time: 37.6 us; the launch traced here: 37.2 us
  Pallas kernels  35.9 us (95%)
  local copies, waits for them, and re-layouts  1.3 us (3%)
    pallas_call x1, Pallas kernels, shards(): pl.pallas_call(kernel, name='attend_and_project', out_shape=jax.ShapeDtyp...  35.9 us
    unnamed x11, local copies, waits for them, and re-layouts  1.3 us

profile of v7, /device:TPU:1, one launch (start us, length us, event | category | flops | bytes accessed | tf_op | source)
XLA Modules:
  0.0 37.2 jit_solution(3337161432632953244)
XLA Ops:
  0.0 0.0 copy-start.3
  0.0 0.0 copy-start.4
  0.0 0.0 copy-start
  0.0 0.0 copy-start.1
  0.0 0.0 copy-start.2
  0.0 0.6 %copy-done.3 = bf16[1,128]{1,0:T(2,128)(2,1)S(1)} copy-done((bf16[1,128]{1,0:T(2,128)(2,1)S(1)}, bf16[1,128]{1,0:T(2,128)(2,1)}, u32[]{:S(2)}) %copy-start.3) | copy-done | bytes 280
  0.7 0.0 copy-done.4
  0.7 0.0 copy-done
  0.7 0.0 copy-done.1
  0.7 0.0 copy-done.2
  0.7 35.9 %attend_and_project.1 = bf16[8,192]{1,0:T(8,128)(2,1)S(1)} custom-call(bf16[1,768]{1,0:T(2,128)(2,1)S(1)} %copy-done, bf16[1,128]{1,0:T(2,128)(2,1)S(1)} %copy-done.2, bf16[1,128]{1,0:T(2,128)(2,1)S(1)} %copy-done.3, bf16[8,256,128]{2,1,0:T(8,128)(2,1)} %bitcast.5, bf16[8,256,128]{2,1,0:T(8,128)(2,1)} %bitcast.6, s32[2,256]{1,0:T(2,128)S(1)} %copy-done.1, ...), custom_call_target="tpu_custom_call" | custom-call | tf_op jit(solution)/shard_map/attend_and_project/pallas_call | solution.py:434
  36.6 0.6 %copy.10 = bf16[8,192]{1,0:T(8,128)(2,1)} copy(bf16[8,192]{1,0:T(8,128)(2,1)S(1)} %attend_and_project.1) | data formatting | bytes 6144
Async XLA Ops:
  0.0 0.7 %copy-start.3 = (bf16[1,128]{1,0:T(2,128)(2,1)S(1)}, bf16[1,128]{1,0:T(2,128)(2,1)}, u32[]{:S(2)}) copy-start(bf16[1,128]{1,0:T(2,128)(2,1)} %sv_hbm.1) | copy-start | bytes 772
  0.0 0.7 %copy-start.4 = (s32[2]{0:T(128)S(1)}, s32[2]{0:T(128)}, u32[]{:S(2)}) copy-start(s32[2]{0:T(128)} %param.14) | copy-start | bytes 28
  0.0 0.7 %copy-start = (bf16[1,768]{1,0:T(2,128)(2,1)S(1)}, bf16[1,768]{1,0:T(2,128)(2,1)}, u32[]{:S(2)}) copy-start(bf16[1,768]{1,0:T(2,128)(2,1)} %q_hbm.1) | copy-start | bytes 4612
  0.0 0.7 %copy-start.1 = (s32[2,256]{1,0:T(2,128)S(1)}, s32[2,256]{1,0:T(2,128)}, u32[]{:S(2)}) copy-start(s32[2,256]{1,0:T(2,128)} %slot_hbm.1) | copy-start | bytes 6148
  0.0 0.7 %copy-start.2 = (bf16[1,128]{1,0:T(2,128)(2,1)S(1)}, bf16[1,128]{1,0:T(2,128)(2,1)}, u32[]{:S(2)}) copy-start(bf16[1,128]{1,0:T(2,128)(2,1)} %sk_hbm.1) | copy-start | bytes 772
